TPU v7x, 32 devices: a whole 2x2x4 slice. The times are simulated.
32 devices in a mesh: rep: 8 (over y, x, core), blk: 4 (over z).
Axes of the slice: x: 2, y: 2, z: 4, core: 2. Of those that a mesh axis runs over, the one named last changes fastest.
Arguments:
- green_samples: bfloat16 [128, 2, 128, 128], P(('rep', 'blk')), may hold values from -0.4453125 to 0.4453125
- exchange_index_order: int32 [16, 128], P('blk'), may hold values from 0 to 127, each once within a row
- frequency_offset: int32 [16], P('blk'), may hold values from 0 to 127
Outputs:
- vertex: float32 [2, 16, 128, 128], P(None, 'blk', 'rep')
Inputs may be any that keep to these rules, and one draw needn't show every extreme that they name: Each row of exchange_index_order names every index of 0 to 127 once.
All inputs are finite; a program needn't handle non-finite values.
Results may differ from a plain program's by a relative error of at most 0.0003.
Values may be sent and summed in bfloat16 or wider, within the bound.
No kernel may reach another device: no remote copies, remote signals or barrier semaphores. Data moves between devices by JAX's collectives and lax.ppermute only.
A program may use at most 128 MiB of HBM per device.

v0:
```python
import jax
import jax.numpy as jnp
from jax import lax
from jax.sharding import PartitionSpec as P


def body(green_samples, exchange_index_order, frequency_offset):
    tile_width = green_samples.shape[2]
    positions = jnp.arange(tile_width, dtype=jnp.int32)
    back_rows = (positions[None, :] - frequency_offset[:, None]) % tile_width
    composed_cols = jnp.take_along_axis(exchange_index_order, back_rows, axis=1)
    left_table = (composed_cols[:, None, :] == positions[None, :, None]).astype(jnp.bfloat16)
    tile_portion = lax.all_gather(green_samples, "blk", axis=0, tiled=True)
    left = jnp.einsum(
        "mcis,qsk->mciqk", tile_portion, left_table, preferred_element_type=jnp.float32
    ).astype(jnp.bfloat16)
    real_part = jnp.einsum(
        "miqk,mkj->qij", left[:, 0], tile_portion[:, 0], preferred_element_type=jnp.float32
    )
    real_part = real_part - jnp.einsum(
        "miqk,mkj->qij", left[:, 1], tile_portion[:, 1], preferred_element_type=jnp.float32
    )
    imag_part = jnp.einsum(
        "miqk,mkj->qij", left[:, 0], tile_portion[:, 1], preferred_element_type=jnp.float32
    )
    imag_part = imag_part + jnp.einsum(
        "miqk,mkj->qij", left[:, 1], tile_portion[:, 0], preferred_element_type=jnp.float32
    )
    real_part, imag_part = (real_part, imag_part)
    stacked = jnp.stack([real_part, imag_part])
    return lax.psum_scatter(stacked, "rep", scatter_dimension=2, tiled=True)


def solution(mesh):
    placed = (P(("rep", "blk"), None, None, None), P("blk", None), P("blk"))
    return jax.shard_map(
        body, mesh=mesh, in_specs=placed, out_specs=P(None, "blk", "rep", None), check_vma=False
    )
```

profile of v0, /device:TPU:0, one launch (start us, length us, event | category | flops | bytes accessed | tf_op | source)
XLA Modules:
  0.0 86.7 jit_solution(18320953328996201132)
XLA Ops:
  6.5 0.0 copy-start
  6.5 0.0 all-gather.2.cloned.1.call-start
  6.5 0.7 all-gather.2.cloned.1.call-update
  7.3 0.0 reduce-scatter.2.cloned.1.call-start
  7.3 0.7 fusion.21
  8.0 0.0 copy-done
  8.1 4.7 %gather_fusion = s32[512]{0:T(512)S(1)} fusion(s32[4,128]{1,0:T(4,128)S(1)} %copy-done, s32[512]{0:T(512)S(1)} %fusion.21), kind=kCustom, calls=%fused_computation | custom fusion | bytes 8192 | tf_op jit(solution)/shard_map/jit(take_along_axis)/gather | solution.py:11
  12.7 0.7 bitcast_select_fusion
  13.5 26.1 %all-gather.2.cloned.1.call-done = bf16[16,2,128,128]{3,2,1,0:T(8,128)(2,1)} async-done(((bf16[4,2,128,128]{3,2,1,0:T(8,128)(2,1)}), bf16[16,2,128,128]{3,2,1,0:T(8,128)(2,1)}) %all-gather.2.cloned.1.call-update) | async-done | bytes 1048592 | tf_op jit(solution)/shard_map/all_gather | solution.py:13
  39.6 0.0 copy-start.1
  39.6 2.6 %convert_bitcast_fusion = bf16[16,2,128,4,128]{2,4,1,0,3:T(8,128)(2,1)S(1)} fusion(bf16[16,2,128,128]{3,2,1,0:T(8,128)(2,1)} %all-gather.2.cloned.1.call-done, s32[4,128]{1,0:T(4,128)S(1)} %bitcast_select_fusion), kind=kOutput, calls=%fused_computation.1 | convolution fusion | flops 539033600 | bytes 5244928 | tf_op jit(solution)/shard_map/mcis,qsk->mciqk/dot_general | solution.py:14
  42.2 0.0 copy-done.1
  42.2 0.7 fusion.5
  43.0 0.7 fusion.4
  43.7 0.8 fusion.9
  44.5 0.7 fusion.11
  45.2 0.8 pad_maximum_fusion
  46.0 0.0 reduce-scatter.2.cloned.1.call-update
  46.1 33.8 %reduce-scatter.2.cloned.1.call-done = f32[2,4,16,128]{3,2,1,0:T(8,128)} async-done(((f32[2,4,128,128]{3,2,1,0:T(8,128)}), f32[2,4,16,128]{3,2,1,0:T(8,128)}) %reduce-scatter.2.cloned.1.call-update) | async-done | bytes 65552 | tf_op jit(solution)/shard_map/reduce_scatter | solution.py:31
Async XLA Ops:
  6.5 1.5 %copy-start = (s32[4,128]{1,0:T(4,128)S(1)}, s32[4,128]{1,0:T(4,128)}, u32[]{:S(2)}) copy-start(s32[4,128]{1,0:T(4,128)} %param.4) | copy-start | bytes 6148
  6.5 33.1 %all-gather.2.cloned.1.call-start = ((), (), s32[]{:S(2)}) async-start(), calls=%async_computation.1 | async-start | bytes 1310720 | tf_op jit(solution)/shard_map/all_gather | solution.py:13
  7.3 72.6 %reduce-scatter.2.cloned.1.call-start = ((), (), s32[]{:S(2)}) async-start(), calls=%async_computation.2 | async-start | bytes 589824 | tf_op jit(solution)/shard_map/reduce_scatter | solution.py:31
  39.6 2.6 %copy-start.1 = (bf16[16,2,128,128]{3,2,1,0:T(8,128)(2,1)S(1)}, bf16[16,2,128,128]{3,2,1,0:T(8,128)(2,1)}, u32[]{:S(2)}) copy-start(bf16[16,2,128,128]{3,2,1,0:T(8,128)(2,1)} %all-gather.2.cloned.1.call-done) | copy-start | bytes 3145732
Sparse Core Ops, SparseCore 0:
  8.9 30.6 all-gather.1
  46.2 33.6 reduce-scatter.1
where the time goes:
time: 86.8 us; the launch traced here: 86.7 us
  waiting for transfers between devices  60.6 us (70%)
  between operations  13.4 us (15%)
  matrix products  5.59 us (6%)
  local copies, waits for them, and re-layouts  4.68 us (5%)
  other arithmetic  2.3 us (3%)
    reduce_scatter x1, waiting for transfers between devices, body(): return lax.psum_scatter(stacked, 'rep', scatter_dimension=2, tiled=True)  33.8 us
    all_gather x1, waiting for transfers between devices, body(): tile_portion = lax.all_gather(green_samples, 'blk', axis=0, tiled=True)  26.1 us
    gather x1, local copies, waits for them, and re-layouts, body(): composed_cols = jnp.take_along_axis(exchange_index_order, back_rows, axis=1)  4.67 us
    dot_general x1, matrix products, body(): jnp.einsum('mcis,qsk->mciqk', tile_portion, left_table, preferred_element...  2.6 us
  transfers between devices with their start and end apart: 2, of which 2 were waited for; matrix products, arithmetic and copies ran while one was open for 7% of the time, Pallas kernels for 0%

commit v1 on v0

v1 whole, which is shorter than its diff:
```python
import functools

import jax
import jax.numpy as jnp
from jax import lax
from jax.experimental import pallas as pl
from jax.experimental.pallas import tpu as pltpu
from jax.sharding import PartitionSpec as P

VMEM_BYTES = 48 * 1024 * 1024


def plain_body(green_samples, exchange_index_order, frequency_offset):
    tile_width = green_samples.shape[2]
    positions = jnp.arange(tile_width, dtype=jnp.int32)
    back_rows = (positions[None, :] - frequency_offset[:, None]) % tile_width
    composed_cols = jnp.take_along_axis(exchange_index_order, back_rows, axis=1)
    left_table = (composed_cols[:, None, :] == positions[None, :, None]).astype(jnp.bfloat16)
    tile_portion = lax.all_gather(green_samples, "blk", axis=0, tiled=True)
    left = jnp.einsum(
        "mcis,qsk->mciqk", tile_portion, left_table, preferred_element_type=jnp.float32
    ).astype(jnp.bfloat16)
    dot = functools.partial(jnp.einsum, "miqk,mkj->qij", preferred_element_type=jnp.float32)
    real_part = dot(left[:, 0], tile_portion[:, 0]) - dot(left[:, 1], tile_portion[:, 1])
    imag_part = dot(left[:, 0], tile_portion[:, 1]) + dot(left[:, 1], tile_portion[:, 0])
    stacked = jnp.stack([real_part, imag_part])
    return lax.psum_scatter(stacked, "rep", scatter_dimension=2, tiled=True)


def partial_tiles_kernel(
    rep, rows, tiles, order_refs, shift_refs, sample_refs, sum_in, out_refs, table, picked, left, right, total
):
    width = table.shape[0]
    mine = lax.axis_index("rep")
    owners = rep // 2
    block = owners * rows
    columns = lax.broadcasted_iota(jnp.int32, (width, width), 0)
    for group, (order, shift) in enumerate(zip(order_refs, shift_refs)):
        names = order[...]
        for tile in range(tiles):
            turned = pltpu.roll(names, shift[tiles + tile, 0], 1)[tile : tile + 1, :]
            place = (group * tiles + tile) * width
            hot = jnp.where(columns == turned, 1.0, 0.0).astype(jnp.bfloat16)
            table[:, place : place + width] = hot
    count = sample_refs[0].shape[0]
    tile_count = len(order_refs) * tiles
    for source, samples in enumerate(sample_refs):
        for sample in range(count):
            at = source * count + sample
            for part in range(2):
                for step in range(owners):
                    owner = (((mine // 2) ^ step) * 2 + mine % 2) * rows
                    picked[part * block + step * rows : part * block + (step + 1) * rows, :] = samples[
                        sample, part, pl.ds(pl.multiple_of(owner, rows), rows), :
                    ]
            real, imag = samples[sample, 0], samples[sample, 1]
            deep = at * 2 * width
            right[deep : deep + width, :width] = real
            right[deep : deep + width, width:] = imag
            right[deep + width : deep + 2 * width, :width] = -imag
            right[deep + width : deep + 2 * width, width:] = real
            moved = jnp.dot(picked[...], table[...], preferred_element_type=jnp.float32).astype(jnp.bfloat16)
            for tile in range(tile_count):
                for part in range(2):
                    left[tile * block : (tile + 1) * block, deep + part * width : deep + (part + 1) * width] = moved[
                        part * block : (part + 1) * block, tile * width : (tile + 1) * width
                    ]
    sums = jnp.dot(left[...], right[...], preferred_element_type=jnp.float32)
    if sum_in is not None:
        sums = sums + sum_in[...]
    total[...] = sums
    if out_refs is not None:
        for group in range(len(order_refs)):
            for step in range(owners):
                for tile in range(tiles):
                    start = (group * tiles + tile) * block + step * rows
                    out_refs[group][step][tile * rows : (tile + 1) * rows, :] = total[start : start + rows, :]


def partial_tiles(rep, rows, tiles, packs, sources, sum_in, last):
    groups, owners = len(packs), rep // 2
    width = packs[0].shape[1]
    count = sources[0].shape[0]
    depth = len(sources) * count * 2 * width
    block = owners * rows
    height = groups * tiles * block

    def kernel(*refs):
        refs = list(refs)
        orders = [refs.pop(0) for _ in range(groups)]
        shifts = [refs.pop(0) for _ in range(groups)]
        samples = [refs.pop(0) for _ in sources]
        before = refs.pop(0) if sum_in is not None else None
        outs = None
        if last:
            outs = [[refs.pop(0) for _ in range(owners)] for _ in range(groups)]
            total = refs.pop()
        else:
            total = refs.pop(0)
        partial_tiles_kernel(rep, rows, tiles, orders, shifts, samples, before, outs, *refs, total)

    scratch = [
        pltpu.VMEM((width, groups * tiles * width), jnp.bfloat16),
        pltpu.VMEM((2 * block, width), jnp.bfloat16),
        pltpu.VMEM((height, depth), jnp.bfloat16),
        pltpu.VMEM((depth, 2 * width), jnp.bfloat16),
    ]
    if last:
        out_shape = [jax.ShapeDtypeStruct((tiles * rows, 2 * width), jnp.float32)] * (groups * owners)
        scratch.append(pltpu.VMEM((height, 2 * width), jnp.float32))
    else:
        out_shape = [jax.ShapeDtypeStruct((height, 2 * width), jnp.float32)]
    whole = pl.BlockSpec(memory_space=pltpu.VMEM)
    scalars = pl.BlockSpec(memory_space=pltpu.SMEM)
    sums = [] if sum_in is None else [sum_in]
    in_specs = [whole] * groups + [scalars] * groups + [whole] * (len(sources) + len(sums))
    got = pl.pallas_call(
        kernel,
        out_shape=out_shape,
        in_specs=in_specs,
        out_specs=[whole] * len(out_shape),
        scratch_shapes=scratch,
        compiler_params=pltpu.CompilerParams(vmem_limit_bytes=VMEM_BYTES),
        cost_estimate=pl.CostEstimate(
            flops=2 * height * depth * 2 * width * 2, bytes_accessed=2 * depth * width, transcendentals=0
        ),
    )(*packs, *packs, *sources, *sums)
    if not last:
        return got[0]
    return [got[group * owners : (group + 1) * owners] for group in range(groups)]


def body(rep, blk, green_samples, exchange_index_order, frequency_offset):
    tiles, width = exchange_index_order.shape
    rows = width // rep

    def over(axis, size, flip, value):
        return lax.ppermute(value, axis, [(i, i ^ flip) for i in range(size)])

    pack = jnp.concatenate(
        [exchange_index_order, jnp.broadcast_to(frequency_offset[:, None], (tiles, width))]
    )
    near = over("blk", blk, 1, green_samples)
    far_pack = over("blk", blk, 2, pack)
    twin = over("rep", rep, 1, green_samples)
    near_twin = over("rep", rep, 1, near)
    packs = [far_pack, pack]
    sums = partial_tiles(rep, rows, tiles, packs, [green_samples, twin], None, False)
    far_parts, own_parts = partial_tiles(rep, rows, tiles, packs, [near, near_twin], sums, True)

    def collect(parts):
        value = parts[0]
        for step in range(1, rep // 2):
            value = value + over("rep", rep, 2 * step, parts[step])
        return value

    far = over("blk", blk, 2, collect(far_parts))
    done = collect(own_parts) + far
    done = done.reshape(tiles, rows, 2, width)
    return jnp.transpose(done, (2, 0, 1, 3))


def solution(mesh):
    rep, blk = mesh.shape["rep"], mesh.shape["blk"]
    placed = (P(("rep", "blk"), None, None, None), P("blk", None), P("blk"))

    def program(green_samples, exchange_index_order, frequency_offset):
        width = exchange_index_order.shape[1]
        if blk == 4 and width // rep % 16 == 0:
            part = functools.partial(body, rep, blk)
        else:
            part = plain_body
        return jax.shard_map(
            part, mesh=mesh, in_specs=placed, out_specs=P(None, "blk", "rep", None), check_vma=False
        )(green_samples, exchange_index_order, frequency_offset)

    return program
```

time: 86.8 us -> 34.9 us (0.40)
  waiting for transfers between devices: 60.6 us -> 11.2 us
  starting transfers between devices: 0.04 us -> 16.1 us
  between operations: 13.4 us -> 0.05 us
  matrix products: 5.59 us -> 0 us
  Pallas kernels: 0 us -> 4.32 us
  local copies, waits for them, and re-layouts: 4.68 us -> 2.35 us
  other arithmetic: 2.3 us -> 0.79 us
    reduce_scatter x1 -> x0, waiting for transfers between devices: 33.8 us -> none  [body(): return lax.psum_scatter(stacked, 'rep', scatter_dimension=2, tiled=True)]
    all_gather x1 -> x0, waiting for transfers between devices: 26.1 us -> none  [body(): tile_portion = lax.all_gather(green_samples, 'blk', axis=0, tiled=True)]
    ppermute x0 -> x11, starting transfers between devices: none -> 16.1 us  [over(): return lax.ppermute(value, axis, [(i, i ^ flip) for i in range(size)])]
    ppermute x0 -> x11, waiting for transfers between devices: none -> 11.2 us  [over(): return lax.ppermute(value, axis, [(i, i ^ flip) for i in range(size)])]
    dot_general x5 -> x0, matrix products: 5.59 us -> none  [the longest x1 2.6 us: body(): jnp.einsum('mcis,qsk->mciqk', tile_portion, left_table, preferred_element...]
    gather x1 -> x0, local copies, waits for them, and re-layouts: 4.67 us -> none  [body(): composed_cols = jnp.take_along_axis(exchange_index_order, back_rows, axis=1)]
    pallas_call x0 -> x2, Pallas kernels: none -> 4.32 us  [partial_tiles(): pl.pallas_call(kernel, out_shape=out_shape, in_specs=in_specs, out_specs=...]
    unnamed x4 -> x2, local copies, waits for them, and re-layouts: 0.01 us -> 0.95 us
  transfers between devices with their start and end apart: 2 -> 11, of which waited for: 2 -> 5; matrix products, arithmetic and copies ran while one was open for 7% -> 4% of each run, Pallas kernels for 0% -> 6%
where the time goes in v1:
time: 34.9 us; the launch traced here: 34.8 us
  starting transfers between devices  16.1 us (46%)
  waiting for transfers between devices  11.2 us (32%)
  Pallas kernels  4.32 us (12%)
  local copies, waits for them, and re-layouts  2.35 us (7%)
  other arithmetic  0.79 us (2%)
    ppermute x11, starting transfers between devices, over(): return lax.ppermute(value, axis, [(i, i ^ flip) for i in range(size)])  16.1 us
    ppermute x11, waiting for transfers between devices, over(): return lax.ppermute(value, axis, [(i, i ^ flip) for i in range(size)])  11.2 us
    pallas_call x2, Pallas kernels, partial_tiles(): pl.pallas_call(kernel, out_shape=out_shape, in_specs=in_specs, out_specs=...  4.32 us
    unnamed x2, local copies, waits for them, and re-layouts  0.95 us
    concatenate x1, other arithmetic, body(): jnp.concatenate([exchange_index_order, jnp.broadcast_to(frequency_offset[...  0.75 us
    concatenate x1, local copies, waits for them, and re-layouts, body(): jnp.concatenate([exchange_index_order, jnp.broadcast_to(frequency_offset[...  0.73 us
  transfers between devices with their start and end apart: 11, of which 5 were waited for; matrix products, arithmetic and copies ran while one was open for 4% of the time, Pallas kernels for 6%

profile of v1, /device:TPU:0, one launch (start us, length us, event | category | flops | bytes accessed | tf_op | source)
XLA Modules:
  0.0 34.8 jit_solution(2887247654247454628)
XLA Ops:
  0.0 3.0 %collective-permute-start.1 = (bf16[4,2,128,128]{3,2,1,0:T(8,128)(2,1)}, bf16[4,2,128,128]{3,2,1,0:T(8,128)(2,1)S(1)}, u32[]{:S(2)}, u32[]{:S(2)}) collective-permute-start(bf16[4,2,128,128]{3,2,1,0:T(8,128)(2,1)} %refs_4_.1), channel_id=1, source_target_pairs={{0,1},{1,0},{2,3},{3,2},{4,5},{5,4},{6,7},{7,6},{8,9},{9,8},{10,11... | collective-permute-start | bytes 786440 | tf_op jit(solution)/shard_map/ppermute | solution.py:138
  3.0 0.0 collective-permute-start.3
  3.0 0.7 %pad.1.clone = s32[8]{0:T(128)S(1)} pad(s32[4]{0:T(128)} %param.5, s32[]{:T(128)} %constant.1), padding=4_0 | pad | bytes 52 | tf_op jit(solution)/shard_map/concatenate | solution.py:140
  3.8 5.8 %collective-permute-done.1.refs_4_ = bf16[4,2,128,128]{3,2,1,0:T(8,128)(2,1)S(1)} collective-permute-done((bf16[4,2,128,128]{3,2,1,0:T(8,128)(2,1)}, bf16[4,2,128,128]{3,2,1,0:T(8,128)(2,1)S(1)}, u32[]{:S(2)}, u32[]{:S(2)}) %collective-permute-start.1) | collective-permute-done | bytes 262176 | tf_op jit(solution)/shard_map/ppermute | solution.py:138
  9.5 0.0 collective-permute-start.2
  9.5 0.8 %pad_add_fusion.refs_1_.refs_3_ = s32[8,128]{1,0:T(8,128)S(1)} fusion(s32[4,128]{1,0:T(4,128)} %param.4, s32[8]{0:T(128)S(1)} %pad.1.clone), kind=kLoop, calls=%fused_computation.3 | loop fusion | flops 1024 | bytes 6176 | tf_op jit(solution)/shard_map/concatenate | solution.py:140
  10.3 2.8 %collective-permute-start = (s32[8,128]{1,0:T(8,128)S(1)}, s32[8,128]{1,0:T(8,128)S(1)}, u32[]{:S(2)}, u32[]{:S(2)}) collective-permute-start(s32[8,128]{1,0:T(8,128)S(1)} %pad_add_fusion.refs_1_.refs_3_), channel_id=1, source_target_pairs={{0,2},{1,3},{2,0},{3,1},{4,6},{5,7},{6,4},{7,5},{8,10},{9,11},{10,... | collective-permute-start | bytes 12296 | tf_op jit(solution)/shard_map/ppermute | solution.py:138
  13.0 1.8 %collective-permute-done.refs_0_.refs_2_ = s32[8,128]{1,0:T(8,128)S(1)} collective-permute-done((s32[8,128]{1,0:T(8,128)S(1)}, s32[8,128]{1,0:T(8,128)S(1)}, u32[]{:S(2)}, u32[]{:S(2)}) %collective-permute-start) | collective-permute-done | bytes 4128 | tf_op jit(solution)/shard_map/ppermute | solution.py:138
  14.8 0.0 collective-permute-done.3.refs_5_
  14.8 0.0 copy-start
  14.8 0.9 %copy-done = bf16[4,2,128,128]{3,2,1,0:T(8,128)(2,1)S(1)} copy-done((bf16[4,2,128,128]{3,2,1,0:T(8,128)(2,1)S(1)}, bf16[4,2,128,128]{3,2,1,0:T(8,128)(2,1)}, u32[]{:S(2)}) %copy-start) | copy-done | bytes 262168
  15.8 2.1 %shard_map.37.refs_6_ = f32[512,256]{1,0:T(8,128)S(1)} custom-call(s32[8,128]{1,0:T(8,128)S(1)} %collective-permute-done.refs_0_.refs_2_, s32[8,128]{1,0:T(8,128)S(1)} %pad_add_fusion.refs_1_.refs_3_, s32[8,128]{1,0:T(8,128)S(1)} %collective-permute-done.refs_0_.refs_2_, s32[8,128]{1,0:T(8,128)S(1)} %pad_add_fusion.refs_1_.refs_3_, ...), custom_call_target="tpu_custom_call" | custom-call | flops 1073741824 | bytes 524288 | tf_op jit(solution)/shard_map/pallas_call | solution.py:117
  17.9 0.0 collective-permute-done.2.refs_5_
  17.9 2.2 %shard_map.38 = (f32[64,256]{1,0:T(8,128)S(1)}, f32[64,256]{1,0:T(8,128)S(1)}, f32[64,256]{1,0:T(8,128)S(1)}, f32[64,256]{1,0:T(8,128)S(1)}, f32[64,256]{1,0:T(8...) custom-call(s32[8,128]{1,0:T(8,128)S(1)} %collective-permute-done.refs_0_.refs_2_, ...), custom_call_target="tpu_custom_call" | custom-call | flops 1073741824 | bytes 524288 | tf_op jit(solution)/shard_map/pallas_call | solution.py:117
  20.1 1.7 %collective-permute-start.7 = (f32[64,256]{1,0:T(8,128)S(1)}, f32[64,256]{1,0:T(8,128)S(1)}, u32[]{:S(2)}, u32[]{:S(2)}) collective-permute-start(f32[64,256]{1,0:T(8,128)S(1)} %get-tuple-element.18), channel_id=1, source_target_pairs={{0,8},{4,12},{8,0},{12,4},{16,24},{20,28},{24,16},{28,20},{1,9},{5... | collective-permute-start | bytes 196616 | tf_op jit(solution)/shard_map/ppermute | solution.py:138
  21.8 1.5 %collective-permute-start.8 = (f32[64,256]{1,0:T(8,128)S(1)}, f32[64,256]{1,0:T(8,128)S(1)}, u32[]{:S(2)}, u32[]{:S(2)}) collective-permute-start(f32[64,256]{1,0:T(8,128)S(1)} %get-tuple-element.19), channel_id=1, source_target_pairs={{0,16},{4,20},{8,24},{12,28},{16,0},{20,4},{24,8},{28,12},{1,17},{... | collective-permute-start | bytes 196616 | tf_op jit(solution)/shard_map/ppermute | solution.py:138
  23.4 0.3 collective-permute-start.9
  23.7 1.7 %collective-permute-start.4 = (f32[64,256]{1,0:T(8,128)S(1)}, f32[64,256]{1,0:T(8,128)S(1)}, u32[]{:S(2)}, u32[]{:S(2)}) collective-permute-start(f32[64,256]{1,0:T(8,128)S(1)} %get-tuple-element.14), channel_id=1, source_target_pairs={{0,8},{4,12},{8,0},{12,4},{16,24},{20,28},{24,16},{28,20},{1,9},{5... | collective-permute-start | bytes 196616 | tf_op jit(solution)/shard_map/ppermute | solution.py:138
  25.3 1.5 %collective-permute-start.5 = (f32[64,256]{1,0:T(8,128)S(1)}, f32[64,256]{1,0:T(8,128)S(1)}, u32[]{:S(2)}, u32[]{:S(2)}) collective-permute-start(f32[64,256]{1,0:T(8,128)S(1)} %get-tuple-element.15), channel_id=1, source_target_pairs={{0,16},{4,20},{8,24},{12,28},{16,0},{20,4},{24,8},{28,12},{1,17},{... | collective-permute-start | bytes 196616 | tf_op jit(solution)/shard_map/ppermute | solution.py:138
  26.8 0.0 collective-permute-done.7
  26.8 0.9 %collective-permute-start.6 = (f32[64,256]{1,0:T(8,128)S(1)}, f32[64,256]{1,0:T(8,128)S(1)}, u32[]{:S(2)}, u32[]{:S(2)}) collective-permute-start(f32[64,256]{1,0:T(8,128)S(1)} %get-tuple-element.16), channel_id=1, source_target_pairs={{0,24},{4,28},{8,16},{12,20},{16,8},{20,12},{24,0},{28,4},{1,25},{... | collective-permute-start | bytes 196616 | tf_op jit(solution)/shard_map/ppermute | solution.py:138
  27.8 0.0 collective-permute-done.8
  27.8 1.1 %collective-permute-done.9 = f32[64,256]{1,0:T(8,128)S(1)} collective-permute-done((f32[64,256]{1,0:T(8,128)S(1)}, f32[64,256]{1,0:T(8,128)S(1)}, u32[]{:S(2)}, u32[]{:S(2)}) %collective-permute-start.9) | collective-permute-done | bytes 65568 | tf_op jit(solution)/shard_map/ppermute | solution.py:138
  28.8 2.7 %collective-permute-start.10 = (f32[64,256]{1,0:T(8,128)S(1)}, f32[64,256]{1,0:T(8,128)S(1)}, u32[]{:S(2)}, u32[]{:S(2)}) collective-permute-start(f32[64,256]{1,0:T(8,128)S(1)} %add_add_fusion), channel_id=1, source_target_pairs={{0,2},{1,3},{2,0},{3,1},{4,6},{5,7},{6,4},{7,5},{8,10},{9,11},{10,... | collective-permute-start | bytes 196616 | tf_op jit(solution)/shard_map/ppermute | solution.py:138
  31.5 0.0 collective-permute-done.4
  31.5 0.0 collective-permute-done.5
  31.5 0.5 %collective-permute-done.6 = f32[64,256]{1,0:T(8,128)S(1)} collective-permute-done((f32[64,256]{1,0:T(8,128)S(1)}, f32[64,256]{1,0:T(8,128)S(1)}, u32[]{:S(2)}, u32[]{:S(2)}) %collective-permute-start.6) | collective-permute-done | bytes 65568 | tf_op jit(solution)/shard_map/ppermute | solution.py:138
  32.0 2.1 %collective-permute-done.10 = f32[64,256]{1,0:T(8,128)S(1)} collective-permute-done((f32[64,256]{1,0:T(8,128)S(1)}, f32[64,256]{1,0:T(8,128)S(1)}, u32[]{:S(2)}, u32[]{:S(2)}) %collective-permute-start.10) | collective-permute-done | bytes 65568 | tf_op jit(solution)/shard_map/ppermute | solution.py:138
  34.1 0.6 %copy.6 = f32[4,16,2,128]{3,1,0,2:T(8,128)} copy(f32[4,16,2,128]{3,2,1,0:T(2,128)S(1)} %reshape.4) | data formatting | bytes 131072 | tf_op jit(solution)/shard_map/reshape | solution.py:159
  (3 shorter events, 0.1 us)
Async XLA Ops:
  0.0 9.5 %collective-permute-start.1 = (bf16[4,2,128,128]{3,2,1,0:T(8,128)(2,1)}, bf16[4,2,128,128]{3,2,1,0:T(8,128)(2,1)S(1)}, u32[]{:S(2)}, u32[]{:S(2)}) collective-permute-start(bf16[4,2,128,128]{3,2,1,0:T(8,128)(2,1)} %refs_4_.1), channel_id=1, source_target_pairs={{0,1},{1,0},{2,3},{3,2},{4,5},{5,4},{6,7},{7,6},{8,9},{9,8},{10,11... | collective-permute-start | bytes 786440 | tf_op jit(solution)/shard_map/ppermute | solution.py:138
  3.0 11.8 %collective-permute-start.3 = (bf16[4,2,128,128]{3,2,1,0:T(8,128)(2,1)}, bf16[4,2,128,128]{3,2,1,0:T(8,128)(2,1)S(1)}, u32[]{:S(2)}, u32[]{:S(2)}) collective-permute-start(bf16[4,2,128,128]{3,2,1,0:T(8,128)(2,1)} %refs_4_.1), channel_id=1, source_target_pairs={{0,4},{4,0},{8,12},{12,8},{16,20},{20,16},{24,28},{28,24},{1,5},{5... | collective-permute-start | bytes 786440 | tf_op jit(solution)/shard_map/ppermute | solution.py:138
  9.5 8.4 %collective-permute-start.2 = (bf16[4,2,128,128]{3,2,1,0:T(8,128)(2,1)S(1)}, bf16[4,2,128,128]{3,2,1,0:T(8,128)(2,1)S(1)}, u32[]{:S(2)}, u32[]{:S(2)}) collective-permute-start(bf16[4,2,128,128]{3,2,1,0:T(8,128)(2,1)S(1)} %collective-permute-done.1.refs_4_), channel_id=1, source_target_pairs={{0,4},{4,0},{8,12},{12,8},{16,20},{20,16},{24,28},{28,24},{1,5},{5... | collective-permute-start | bytes 786440 | tf_op jit(solution)/shard_map/ppermute | solution.py:138
  10.3 4.5 %collective-permute-start = (s32[8,128]{1,0:T(8,128)S(1)}, s32[8,128]{1,0:T(8,128)S(1)}, u32[]{:S(2)}, u32[]{:S(2)}) collective-permute-start(s32[8,128]{1,0:T(8,128)S(1)} %pad_add_fusion.refs_1_.refs_3_), channel_id=1, source_target_pairs={{0,2},{1,3},{2,0},{3,1},{4,6},{5,7},{6,4},{7,5},{8,10},{9,11},{10,... | collective-permute-start | bytes 12296 | tf_op jit(solution)/shard_map/ppermute | solution.py:138
  14.8 1.0 %copy-start = (bf16[4,2,128,128]{3,2,1,0:T(8,128)(2,1)S(1)}, bf16[4,2,128,128]{3,2,1,0:T(8,128)(2,1)}, u32[]{:S(2)}) copy-start(bf16[4,2,128,128]{3,2,1,0:T(8,128)(2,1)} %refs_4_.1) | copy-start | bytes 786436
  20.1 6.7 %collective-permute-start.7 = (f32[64,256]{1,0:T(8,128)S(1)}, f32[64,256]{1,0:T(8,128)S(1)}, u32[]{:S(2)}, u32[]{:S(2)}) collective-permute-start(f32[64,256]{1,0:T(8,128)S(1)} %get-tuple-element.18), channel_id=1, source_target_pairs={{0,8},{4,12},{8,0},{12,4},{16,24},{20,28},{24,16},{28,20},{1,9},{5... | collective-permute-start | bytes 196616 | tf_op jit(solution)/shard_map/ppermute | solution.py:138
  21.8 5.9 %collective-permute-start.8 = (f32[64,256]{1,0:T(8,128)S(1)}, f32[64,256]{1,0:T(8,128)S(1)}, u32[]{:S(2)}, u32[]{:S(2)}) collective-permute-start(f32[64,256]{1,0:T(8,128)S(1)} %get-tuple-element.19), channel_id=1, source_target_pairs={{0,16},{4,20},{8,24},{12,28},{16,0},{20,4},{24,8},{28,12},{1,17},{... | collective-permute-start | bytes 196616 | tf_op jit(solution)/shard_map/ppermute | solution.py:138
  23.4 5.5 %collective-permute-start.9 = (f32[64,256]{1,0:T(8,128)S(1)}, f32[64,256]{1,0:T(8,128)S(1)}, u32[]{:S(2)}, u32[]{:S(2)}) collective-permute-start(f32[64,256]{1,0:T(8,128)S(1)} %get-tuple-element.20), channel_id=1, source_target_pairs={{0,24},{4,28},{8,16},{12,20},{16,8},{20,12},{24,0},{28,4},{1,25},{... | collective-permute-start | bytes 196616 | tf_op jit(solution)/shard_map/ppermute | solution.py:138
  23.7 7.8 %collective-permute-start.4 = (f32[64,256]{1,0:T(8,128)S(1)}, f32[64,256]{1,0:T(8,128)S(1)}, u32[]{:S(2)}, u32[]{:S(2)}) collective-permute-start(f32[64,256]{1,0:T(8,128)S(1)} %get-tuple-element.14), channel_id=1, source_target_pairs={{0,8},{4,12},{8,0},{12,4},{16,24},{20,28},{24,16},{28,20},{1,9},{5... | collective-permute-start | bytes 196616 | tf_op jit(solution)/shard_map/ppermute | solution.py:138
  25.3 6.2 %collective-permute-start.5 = (f32[64,256]{1,0:T(8,128)S(1)}, f32[64,256]{1,0:T(8,128)S(1)}, u32[]{:S(2)}, u32[]{:S(2)}) collective-permute-start(f32[64,256]{1,0:T(8,128)S(1)} %get-tuple-element.15), channel_id=1, source_target_pairs={{0,16},{4,20},{8,24},{12,28},{16,0},{20,4},{24,8},{28,12},{1,17},{... | collective-permute-start | bytes 196616 | tf_op jit(solution)/shard_map/ppermute | solution.py:138
  26.8 5.2 %collective-permute-start.6 = (f32[64,256]{1,0:T(8,128)S(1)}, f32[64,256]{1,0:T(8,128)S(1)}, u32[]{:S(2)}, u32[]{:S(2)}) collective-permute-start(f32[64,256]{1,0:T(8,128)S(1)} %get-tuple-element.16), channel_id=1, source_target_pairs={{0,24},{4,28},{8,16},{12,20},{16,8},{20,12},{24,0},{28,4},{1,25},{... | collective-permute-start | bytes 196616 | tf_op jit(solution)/shard_map/ppermute | solution.py:138
  28.8 5.2 %collective-permute-start.10 = (f32[64,256]{1,0:T(8,128)S(1)}, f32[64,256]{1,0:T(8,128)S(1)}, u32[]{:S(2)}, u32[]{:S(2)}) collective-permute-start(f32[64,256]{1,0:T(8,128)S(1)} %add_add_fusion), channel_id=1, source_target_pairs={{0,2},{1,3},{2,0},{3,1},{4,6},{5,7},{6,4},{7,5},{8,10},{9,11},{10,... | collective-permute-start | bytes 196616 | tf_op jit(solution)/shard_map/ppermute | solution.py:138

commit v2 on v0

v2 whole, which is shorter than its diff:
```python
import functools

import jax
import jax.numpy as jnp
from jax import lax
from jax.experimental import pallas as pl
from jax.experimental.pallas import tpu as pltpu
from jax.sharding import PartitionSpec as P

VMEM_BYTES = 48 * 1024 * 1024


def plain_body(green_samples, exchange_index_order, frequency_offset):
    tile_width = green_samples.shape[2]
    positions = jnp.arange(tile_width, dtype=jnp.int32)
    back_rows = (positions[None, :] - frequency_offset[:, None]) % tile_width
    composed_cols = jnp.take_along_axis(exchange_index_order, back_rows, axis=1)
    left_table = (composed_cols[:, None, :] == positions[None, :, None]).astype(jnp.bfloat16)
    tile_portion = lax.all_gather(green_samples, "blk", axis=0, tiled=True)
    left = jnp.einsum(
        "mcis,qsk->mciqk", tile_portion, left_table, preferred_element_type=jnp.float32
    ).astype(jnp.bfloat16)
    dot = functools.partial(jnp.einsum, "miqk,mkj->qij", preferred_element_type=jnp.float32)
    real_part = dot(left[:, 0], tile_portion[:, 0]) - dot(left[:, 1], tile_portion[:, 1])
    imag_part = dot(left[:, 0], tile_portion[:, 1]) + dot(left[:, 1], tile_portion[:, 0])
    stacked = jnp.stack([real_part, imag_part])
    return lax.psum_scatter(stacked, "rep", scatter_dimension=2, tiled=True)


def turned_order(order, offset):
    tiles, _ = order.shape

    def kernel(order_ref, offset_ref, out_ref):
        names = order_ref[...]
        for tile in range(tiles):
            out_ref[tile : tile + 1, :] = pltpu.roll(names, offset_ref[tile], 1)[tile : tile + 1, :]

    return pl.pallas_call(
        kernel,
        out_shape=jax.ShapeDtypeStruct(order.shape, order.dtype),
        in_specs=[pl.BlockSpec(memory_space=pltpu.VMEM), pl.BlockSpec(memory_space=pltpu.SMEM)],
        out_specs=pl.BlockSpec(memory_space=pltpu.VMEM),
    )(order, offset)


def partial_tiles(rep, rows, tiles, groups, sources, split):
    owners = rep // 2
    width = groups[0][0].shape[1]
    count = sources[0].shape[0]
    block = owners * rows
    height = tiles * block
    step_deep = count * 2 * width
    depth = len(sources) * step_deep

    def kernel(*refs):
        refs = list(refs)
        orders = [refs.pop(0) for _ in groups]
        befores = [None if group[1] is None else refs.pop(0) for group in groups]
        samples = [refs.pop(0) for _ in sources]
        outs = [[refs.pop(0) for _ in range(owners if split else 1)] for _ in groups]
        table, picked, left, right, total = refs
        mine = lax.axis_index("rep")
        columns = lax.broadcasted_iota(jnp.int32, (width, width), 0)
        for group, order in enumerate(orders):
            names = order[...]
            for tile in range(tiles):
                place = (group * tiles + tile) * width
                hot = jnp.where(columns == names[tile : tile + 1, :], 1.0, 0.0).astype(jnp.bfloat16)
                table[:, place : place + width] = hot
        for source, sample_ref in enumerate(samples):
            used = [group for group in range(len(groups)) if groups[group][2] <= source]
            for sample in range(count):
                for part in range(2):
                    for step in range(owners):
                        owner = (((mine // 2) ^ step) * 2 + mine % 2) * rows
                        picked[part * block + step * rows : part * block + (step + 1) * rows, :] = sample_ref[
                            sample, part, pl.ds(pl.multiple_of(owner, rows), rows), :
                        ]
                real, imag = sample_ref[sample, 0], sample_ref[sample, 1]
                deep = source * step_deep + sample * 2 * width
                right[deep : deep + width, :width] = real
                right[deep : deep + width, width:] = imag
                right[deep + width : deep + 2 * width, :width] = -imag
                right[deep + width : deep + 2 * width, width:] = real
                for group in used:
                    moved = jnp.dot(
                        picked[...],
                        table[:, group * tiles * width : (group + 1) * tiles * width],
                        preferred_element_type=jnp.float32,
                    ).astype(jnp.bfloat16)
                    for tile in range(tiles):
                        for part in range(2):
                            left[
                                group * height + tile * block : group * height + (tile + 1) * block,
                                deep + part * width : deep + (part + 1) * width,
                            ] = moved[part * block : (part + 1) * block, tile * width : (tile + 1) * width]
        for group, (_, _, first) in enumerate(groups):
            start = first * step_deep
            sums = jnp.dot(
                left[group * height : (group + 1) * height, start:], right[start:, :], preferred_element_type=jnp.float32
            )
            if befores[group] is not None:
                sums = sums + befores[group][...]
            if not split:
                outs[group][0][...] = sums
                continue
            total[...] = sums
            for step in range(owners):
                for tile in range(tiles):
                    at = tile * block + step * rows
                    outs[group][step][tile * rows : (tile + 1) * rows, :] = total[at : at + rows, :]

    if split:
        out_shape = [jax.ShapeDtypeStruct((tiles * rows, 2 * width), jnp.float32)] * (len(groups) * owners)
    else:
        out_shape = [jax.ShapeDtypeStruct((height, 2 * width), jnp.float32)] * len(groups)
    operands = [group[0] for group in groups] + [group[1] for group in groups if group[1] is not None] + sources
    whole = pl.BlockSpec(memory_space=pltpu.VMEM)
    got = pl.pallas_call(
        kernel,
        out_shape=out_shape,
        in_specs=[whole] * len(operands),
        out_specs=[whole] * len(out_shape),
        scratch_shapes=[
            pltpu.VMEM((width, len(groups) * tiles * width), jnp.bfloat16),
            pltpu.VMEM((2 * block, width), jnp.bfloat16),
            pltpu.VMEM((len(groups) * height, depth), jnp.bfloat16),
            pltpu.VMEM((depth, 2 * width), jnp.bfloat16),
            pltpu.VMEM((height, 2 * width), jnp.float32),
        ],
        compiler_params=pltpu.CompilerParams(vmem_limit_bytes=VMEM_BYTES),
        cost_estimate=pl.CostEstimate(
            flops=4 * len(groups) * height * depth * 2 * width, bytes_accessed=2 * depth * width, transcendentals=0
        ),
    )(*operands)
    per = owners if split else 1
    got = [got[group * per : (group + 1) * per] for group in range(len(groups))]
    return got if split else [each[0] for each in got]


def body(rep, blk, green_samples, exchange_index_order, frequency_offset):
    tiles, width = exchange_index_order.shape
    rows = width // rep

    def over(axis, size, flip, value):
        return lax.ppermute(value, axis, [(i, i ^ flip) for i in range(size)])

    part = functools.partial(partial_tiles, rep, rows, tiles)
    near = over("blk", blk, 1, green_samples)
    twin = over("rep", rep, 1, green_samples)
    own_order = turned_order(exchange_index_order, frequency_offset)
    far_order = over("blk", blk, 2, own_order)
    (own,) = part([(own_order, None, 0)], [green_samples, twin], False)
    near, own, far_order = lax.optimization_barrier((near, own, far_order))
    near_twin = over("rep", rep, 1, near)
    far, own = part([(far_order, None, 0), (own_order, own, 2)], [green_samples, twin, near], False)
    (far_parts,) = part([(far_order, far, 0)], [near_twin], True)
    (own_parts,) = part([(own_order, own, 0)], [near_twin], True)

    def collect(parts):
        value = parts[0]
        for step in range(1, rep // 2):
            value = value + over("rep", rep, 2 * step, parts[step])
        return value

    far = over("blk", blk, 2, collect(far_parts))
    done = collect(own_parts) + far
    done = done.reshape(tiles, rows, 2, width)
    return jnp.transpose(done, (2, 0, 1, 3))


def solution(mesh):
    rep, blk = mesh.shape["rep"], mesh.shape["blk"]
    placed = (P(("rep", "blk"), None, None, None), P("blk", None), P("blk"))

    def program(green_samples, exchange_index_order, frequency_offset):
        width = exchange_index_order.shape[1]
        if blk == 4 and width // rep % 16 == 0:
            part = functools.partial(body, rep, blk)
        else:
            part = plain_body
        return jax.shard_map(
            part, mesh=mesh, in_specs=placed, out_specs=P(None, "blk", "rep", None), check_vma=False
        )(green_samples, exchange_index_order, frequency_offset)

    return program
```

time: 86.8 us -> 27.6 us (0.32)
  waiting for transfers between devices: 60.6 us -> 4.66 us
  starting transfers between devices: 0.04 us -> 15.4 us
  between operations: 13.4 us -> 0.07 us
  matrix products: 5.59 us -> 0 us
  Pallas kernels: 0 us -> 4.94 us
  local copies, waits for them, and re-layouts: 4.68 us -> 2.34 us
  other arithmetic: 2.3 us -> 0.04 us
    reduce_scatter x1 -> x0, waiting for transfers between devices: 33.8 us -> none  [body(): return lax.psum_scatter(stacked, 'rep', scatter_dimension=2, tiled=True)]
    all_gather x1 -> x0, waiting for transfers between devices: 26.1 us -> none  [body(): tile_portion = lax.all_gather(green_samples, 'blk', axis=0, tiled=True)]
    ppermute x0 -> x11, starting transfers between devices: none -> 15.4 us  [over(): return lax.ppermute(value, axis, [(i, i ^ flip) for i in range(size)])]
    dot_general x5 -> x0, matrix products: 5.59 us -> none  [the longest x1 2.6 us: body(): jnp.einsum('mcis,qsk->mciqk', tile_portion, left_table, preferred_element...]
    pallas_call x0 -> x5, Pallas kernels: none -> 4.94 us  [the longest x4 3.49 us: partial_tiles(): pl.pallas_call(kernel, out_shape=out_shape, in_specs=[whole] * len(operan...]
    gather x1 -> x0, local copies, waits for them, and re-layouts: 4.67 us -> none  [body(): composed_cols = jnp.take_along_axis(exchange_index_order, back_rows, axis=1)]
    ppermute x0 -> x11, waiting for transfers between devices: none -> 4.66 us  [over(): return lax.ppermute(value, axis, [(i, i ^ flip) for i in range(size)])]
    unnamed x4 -> x6, local copies, waits for them, and re-layouts: 0.01 us -> 1.66 us
  transfers between devices with their start and end apart: 2 -> 11, of which waited for: 2 -> 4; matrix products, arithmetic and copies ran while one was open for 7% -> 0% of each run, Pallas kernels for 0% -> 16%
where the time goes in v2:
time: 27.6 us; the launch traced here: 27.4 us
  starting transfers between devices  15.4 us (56%)
  Pallas kernels  4.94 us (18%)
  waiting for transfers between devices  4.66 us (17%)
  local copies, waits for them, and re-layouts  2.34 us (8%)
    ppermute x11, starting transfers between devices, over(): return lax.ppermute(value, axis, [(i, i ^ flip) for i in range(size)])  15.4 us
    ppermute x11, waiting for transfers between devices, over(): return lax.ppermute(value, axis, [(i, i ^ flip) for i in range(size)])  4.66 us
    pallas_call x4, Pallas kernels, partial_tiles(): pl.pallas_call(kernel, out_shape=out_shape, in_specs=[whole] * len(operan...  3.49 us
    unnamed x6, local copies, waits for them, and re-layouts  1.66 us
    pallas_call x1, Pallas kernels, turned_order(): pl.pallas_call(kernel, out_shape=jax.ShapeDtypeStruct(order.shape, order....  1.45 us
    reshape x2, local copies, waits for them, and re-layouts, body(): done = done.reshape(tiles, rows, 2, width)  0.67 us
  transfers between devices with their start and end apart: 11, of which 4 were waited for; matrix products, arithmetic and copies ran while one was open for 0% of the time, Pallas kernels for 16%

profile of v2, /device:TPU:0, one launch (start us, length us, event | category | flops | bytes accessed | tf_op | source)
XLA Modules:
  0.0 27.4 jit_solution(14987995349518513633)
XLA Ops:
  0.0 0.5 %collective-permute-start.1 = (bf16[4,2,128,128]{3,2,1,0:T(8,128)(2,1)}, bf16[4,2,128,128]{3,2,1,0:T(8,128)(2,1)S(1)}, u32[]{:S(2)}, u32[]{:S(2)}) collective-permute-start(bf16[4,2,128,128]{3,2,1,0:T(8,128)(2,1)} %refs_3_.1), channel_id=1, source_target_pairs={{0,4},{4,0},{8,12},{12,8},{16,20},{20,16},{24,28},{28,24},{1,5},{5... | collective-permute-start | bytes 786440 | tf_op jit(solution)/shard_map/ppermute | solution.py:146
  0.5 2.6 %collective-permute-start = (bf16[4,2,128,128]{3,2,1,0:T(8,128)(2,1)}, bf16[4,2,128,128]{3,2,1,0:T(8,128)(2,1)S(1)}, u32[]{:S(2)}, u32[]{:S(2)}) collective-permute-start(bf16[4,2,128,128]{3,2,1,0:T(8,128)(2,1)} %refs_3_.1), channel_id=1, source_target_pairs={{0,1},{1,0},{2,3},{3,2},{4,5},{5,4},{6,7},{7,6},{8,9},{9,8},{10,11... | collective-permute-start | bytes 786440 | tf_op jit(solution)/shard_map/ppermute | solution.py:146
  3.0 1.4 %shard_map.37.refs_0_.refs_1_ = s32[4,128]{1,0:T(4,128)} custom-call(s32[4,128]{1,0:T(4,128)} %order_ref.1, s32[4]{0:T(128)} %offset_ref.1), custom_call_target="tpu_custom_call" | custom-call | tf_op jit(solution)/shard_map/pallas_call | solution.py:38
  4.5 2.6 %collective-permute-start.2 = (s32[4,128]{1,0:T(4,128)}, s32[4,128]{1,0:T(4,128)S(1)}, u32[]{:S(2)}, u32[]{:S(2)}) collective-permute-start(s32[4,128]{1,0:T(4,128)} %shard_map.37.refs_0_.refs_1_), channel_id=1, source_target_pairs={{0,2},{1,3},{2,0},{3,1},{4,6},{5,7},{6,4},{7,5},{8,10},{9,11},{10,... | collective-permute-start | bytes 6152 | tf_op jit(solution)/shard_map/ppermute | solution.py:146
  7.1 0.0 collective-permute-done.1.refs_2_.refs_4_
  7.1 0.0 copy-start
  7.1 0.7 %copy-done = s32[4,128]{1,0:T(4,128)S(1)} copy-done((s32[4,128]{1,0:T(4,128)S(1)}, s32[4,128]{1,0:T(4,128)}, u32[]{:S(2)}) %copy-start) | copy-done | bytes 2072
  7.8 0.9 %copy-done.2 = bf16[4,2,128,128]{3,2,1,0:T(8,128)(2,1)S(1)} copy-done((bf16[4,2,128,128]{3,2,1,0:T(8,128)(2,1)S(1)}, bf16[4,2,128,128]{3,2,1,0:T(8,128)(2,1)}, u32[]{:S(2)}) %copy-start.2) | copy-done | bytes 262168
  8.7 0.9 %shard_map.38.refs_2_ = f32[256,256]{1,0:T(8,128)S(1)} custom-call(s32[4,128]{1,0:T(4,128)S(1)} %copy-done, bf16[4,2,128,128]{3,2,1,0:T(8,128)(2,1)S(1)} %copy-done.2, bf16[4,2,128,128]{3,2,1,0:T(8,128)(2,1)S(1)} %collective-permute-done.1.refs_2_.refs_4_), custom_call_target="tpu_custom_call" | custom-call | flops 536870912 | bytes 524288 | tf_op jit(solution)/shard_map/pallas_call | solution.py:119
  9.6 0.0 collective-permute-done.2.refs_0_
  9.6 0.6 %collective-permute-done.refs_5_ = bf16[4,2,128,128]{3,2,1,0:T(8,128)(2,1)S(1)} collective-permute-done((bf16[4,2,128,128]{3,2,1,0:T(8,128)(2,1)}, bf16[4,2,128,128]{3,2,1,0:T(8,128)(2,1)S(1)}, u32[]{:S(2)}, u32[]{:S(2)}) %collective-permute-start) | collective-permute-done | bytes 262176 | tf_op jit(solution)/shard_map/ppermute | solution.py:146
  10.3 0.0 collective-permute-start.3
  10.3 0.0 copy-done.1
  10.3 1.5 %shard_map.39 = (f32[256,256]{1,0:T(8,128)S(1)}, f32[256,256]{1,0:T(8,128)S(1)}) custom-call(s32[4,128]{1,0:T(4,128)S(1)} %collective-permute-done.2.refs_0_, s32[4,128]{1,0:T(4,128)S(1)} %copy-done.1, f32[256,256]{1,0:T(8,128)S(1)} %shard_map.38.refs_2_, bf16[4,2,128,128]{3,2,1,0:T(8,128)(2,1)S(1)} %copy-done.2, ...), custom_call_target="tpu_custom_call" | custom-call | flops 1610612736 | bytes 786432 | tf_op jit(solution)/shard_map/pallas_call | solution.py:119
  11.7 0.0 collective-permute-done.3.refs_2_
  11.8 0.6 %shard_map.41 = (f32[64,256]{1,0:T(8,128)S(1)}, f32[64,256]{1,0:T(8,128)S(1)}, f32[64,256]{1,0:T(8,128)S(1)}, f32[64,256]{1,0:T(8,128)S(1)}) custom-call(s32[4,128]{1,0:T(4,128)S(1)} %collective-permute-done.2.refs_0_, f32[256,256]{1,0:T(8,128)S(1)} %get-tuple-element.26.refs_1_, bf16[4,2,128,128]{3,2,1,0:T(8,128)(2,1)S(1)} %collective-permute-done.3.refs_2_), custom_call_target="tpu_custom_call" | custom-call | flops 268435456 | bytes 262144 | tf_op jit(solution)/shard_map/pallas_call | solution.py:119
  12.4 1.7 %collective-permute-start.7 = (f32[64,256]{1,0:T(8,128)S(1)}, f32[64,256]{1,0:T(8,128)S(1)}, u32[]{:S(2)}, u32[]{:S(2)}) collective-permute-start(f32[64,256]{1,0:T(8,128)S(1)} %get-tuple-element.28), channel_id=1, source_target_pairs={{0,8},{4,12},{8,0},{12,4},{16,24},{20,28},{24,16},{28,20},{1,9},{5... | collective-permute-start | bytes 196616 | tf_op jit(solution)/shard_map/ppermute | solution.py:146
  14.1 1.5 %collective-permute-start.8 = (f32[64,256]{1,0:T(8,128)S(1)}, f32[64,256]{1,0:T(8,128)S(1)}, u32[]{:S(2)}, u32[]{:S(2)}) collective-permute-start(f32[64,256]{1,0:T(8,128)S(1)} %get-tuple-element.29), channel_id=1, source_target_pairs={{0,16},{4,20},{8,24},{12,28},{16,0},{20,4},{24,8},{28,12},{1,17},{... | collective-permute-start | bytes 196616 | tf_op jit(solution)/shard_map/ppermute | solution.py:146
  15.6 0.3 %collective-permute-start.9 = (f32[64,256]{1,0:T(8,128)S(1)}, f32[64,256]{1,0:T(8,128)S(1)}, u32[]{:S(2)}, u32[]{:S(2)}) collective-permute-start(f32[64,256]{1,0:T(8,128)S(1)} %get-tuple-element.30), channel_id=1, source_target_pairs={{0,24},{4,28},{8,16},{12,20},{16,8},{20,12},{24,0},{28,4},{1,25},{... | collective-permute-start | bytes 196616 | tf_op jit(solution)/shard_map/ppermute | solution.py:146
  15.9 0.6 %shard_map.40 = (f32[64,256]{1,0:T(8,128)S(1)}, f32[64,256]{1,0:T(8,128)S(1)}, f32[64,256]{1,0:T(8,128)S(1)}, f32[64,256]{1,0:T(8,128)S(1)}) custom-call(s32[4,128]{1,0:T(4,128)S(1)} %copy-done.1, f32[256,256]{1,0:T(8,128)S(1)} %get-tuple-element.21.refs_1_, bf16[4,2,128,128]{3,2,1,0:T(8,128)(2,1)S(1)} %collective-permute-done.3.refs_2_), custom_call_target="tpu_custom_call" | custom-call | flops 268435456 | bytes 262144 | tf_op jit(solution)/shard_map/pallas_call | solution.py:119
  16.5 1.7 %collective-permute-start.4 = (f32[64,256]{1,0:T(8,128)S(1)}, f32[64,256]{1,0:T(8,128)S(1)}, u32[]{:S(2)}, u32[]{:S(2)}) collective-permute-start(f32[64,256]{1,0:T(8,128)S(1)} %get-tuple-element.23), channel_id=1, source_target_pairs={{0,8},{4,12},{8,0},{12,4},{16,24},{20,28},{24,16},{28,20},{1,9},{5... | collective-permute-start | bytes 196616 | tf_op jit(solution)/shard_map/ppermute | solution.py:146
  18.2 1.5 %collective-permute-start.5 = (f32[64,256]{1,0:T(8,128)S(1)}, f32[64,256]{1,0:T(8,128)S(1)}, u32[]{:S(2)}, u32[]{:S(2)}) collective-permute-start(f32[64,256]{1,0:T(8,128)S(1)} %get-tuple-element.24), channel_id=1, source_target_pairs={{0,16},{4,20},{8,24},{12,28},{16,0},{20,4},{24,8},{28,12},{1,17},{... | collective-permute-start | bytes 196616 | tf_op jit(solution)/shard_map/ppermute | solution.py:146
  19.8 0.0 collective-permute-done.7
  19.8 0.3 %collective-permute-start.6 = (f32[64,256]{1,0:T(8,128)S(1)}, f32[64,256]{1,0:T(8,128)S(1)}, u32[]{:S(2)}, u32[]{:S(2)}) collective-permute-start(f32[64,256]{1,0:T(8,128)S(1)} %get-tuple-element.25), channel_id=1, source_target_pairs={{0,24},{4,28},{8,16},{12,20},{16,8},{20,12},{24,0},{28,4},{1,25},{... | collective-permute-start | bytes 196616 | tf_op jit(solution)/shard_map/ppermute | solution.py:146
  20.1 0.0 collective-permute-done.8
  20.1 1.4 %collective-permute-done.9 = f32[64,256]{1,0:T(8,128)S(1)} collective-permute-done((f32[64,256]{1,0:T(8,128)S(1)}, f32[64,256]{1,0:T(8,128)S(1)}, u32[]{:S(2)}, u32[]{:S(2)}) %collective-permute-start.9) | collective-permute-done | bytes 65568 | tf_op jit(solution)/shard_map/ppermute | solution.py:146
  21.5 2.6 %collective-permute-start.10 = (f32[64,256]{1,0:T(8,128)S(1)}, f32[64,256]{1,0:T(8,128)S(1)}, u32[]{:S(2)}, u32[]{:S(2)}) collective-permute-start(f32[64,256]{1,0:T(8,128)S(1)} %add_add_fusion), channel_id=1, source_target_pairs={{0,2},{1,3},{2,0},{3,1},{4,6},{5,7},{6,4},{7,5},{8,10},{9,11},{10,... | collective-permute-start | bytes 196616 | tf_op jit(solution)/shard_map/ppermute | solution.py:146
  24.1 0.0 collective-permute-done.4
  24.1 0.0 collective-permute-done.5
  24.1 0.8 %collective-permute-done.6 = f32[64,256]{1,0:T(8,128)S(1)} collective-permute-done((f32[64,256]{1,0:T(8,128)S(1)}, f32[64,256]{1,0:T(8,128)S(1)}, u32[]{:S(2)}, u32[]{:S(2)}) %collective-permute-start.6) | collective-permute-done | bytes 65568 | tf_op jit(solution)/shard_map/ppermute | solution.py:146
  24.9 1.8 %collective-permute-done.10 = f32[64,256]{1,0:T(8,128)S(1)} collective-permute-done((f32[64,256]{1,0:T(8,128)S(1)}, f32[64,256]{1,0:T(8,128)S(1)}, u32[]{:S(2)}, u32[]{:S(2)}) %collective-permute-start.10) | collective-permute-done | bytes 65568 | tf_op jit(solution)/shard_map/ppermute | solution.py:146
  26.8 0.6 %copy.6 = f32[4,16,2,128]{3,1,0,2:T(8,128)} copy(f32[4,16,2,128]{3,2,1,0:T(2,128)S(1)} %reshape.3) | data formatting | bytes 131072 | tf_op jit(solution)/shard_map/reshape | solution.py:168
  (5 shorter events, 0.1 us)
Async XLA Ops:
  0.0 7.1 %collective-permute-start.1 = (bf16[4,2,128,128]{3,2,1,0:T(8,128)(2,1)}, bf16[4,2,128,128]{3,2,1,0:T(8,128)(2,1)S(1)}, u32[]{:S(2)}, u32[]{:S(2)}) collective-permute-start(bf16[4,2,128,128]{3,2,1,0:T(8,128)(2,1)} %refs_3_.1), channel_id=1, source_target_pairs={{0,4},{4,0},{8,12},{12,8},{16,20},{20,16},{24,28},{28,24},{1,5},{5... | collective-permute-start | bytes 786440 | tf_op jit(solution)/shard_map/ppermute | solution.py:146
  0.5 9.8 %collective-permute-start = (bf16[4,2,128,128]{3,2,1,0:T(8,128)(2,1)}, bf16[4,2,128,128]{3,2,1,0:T(8,128)(2,1)S(1)}, u32[]{:S(2)}, u32[]{:S(2)}) collective-permute-start(bf16[4,2,128,128]{3,2,1,0:T(8,128)(2,1)} %refs_3_.1), channel_id=1, source_target_pairs={{0,1},{1,0},{2,3},{3,2},{4,5},{5,4},{6,7},{7,6},{8,9},{9,8},{10,11... | collective-permute-start | bytes 786440 | tf_op jit(solution)/shard_map/ppermute | solution.py:146
  4.5 5.1 %collective-permute-start.2 = (s32[4,128]{1,0:T(4,128)}, s32[4,128]{1,0:T(4,128)S(1)}, u32[]{:S(2)}, u32[]{:S(2)}) collective-permute-start(s32[4,128]{1,0:T(4,128)} %shard_map.37.refs_0_.refs_1_), channel_id=1, source_target_pairs={{0,2},{1,3},{2,0},{3,1},{4,6},{5,7},{6,4},{7,5},{8,10},{9,11},{10,... | collective-permute-start | bytes 6152 | tf_op jit(solution)/shard_map/ppermute | solution.py:146
  7.1 0.7 %copy-start = (s32[4,128]{1,0:T(4,128)S(1)}, s32[4,128]{1,0:T(4,128)}, u32[]{:S(2)}) copy-start(s32[4,128]{1,0:T(4,128)} %shard_map.37.refs_0_.refs_1_) | copy-start | bytes 6148
  7.8 0.9 %copy-start.2 = (bf16[4,2,128,128]{3,2,1,0:T(8,128)(2,1)S(1)}, bf16[4,2,128,128]{3,2,1,0:T(8,128)(2,1)}, u32[]{:S(2)}) copy-start(bf16[4,2,128,128]{3,2,1,0:T(8,128)(2,1)} %refs_3_.1) | copy-start | bytes 786436
  8.7 1.5 %copy-start.1 = (s32[4,128]{1,0:T(4,128)S(1)}, s32[4,128]{1,0:T(4,128)}, u32[]{:S(2)}) copy-start(s32[4,128]{1,0:T(4,128)} %shard_map.37.refs_0_.refs_1_) | copy-start | bytes 6148
  10.3 1.5 %collective-permute-start.3 = (bf16[4,2,128,128]{3,2,1,0:T(8,128)(2,1)S(1)}, bf16[4,2,128,128]{3,2,1,0:T(8,128)(2,1)S(1)}, u32[]{:S(2)}, u32[]{:S(2)}) collective-permute-start(bf16[4,2,128,128]{3,2,1,0:T(8,128)(2,1)S(1)} %collective-permute-done.refs_5_), channel_id=1, source_target_pairs={{0,4},{4,0},{8,12},{12,8},{16,20},{20,16},{24,28},{28,24},{1,5},{5... | collective-permute-start | bytes 786440 | tf_op jit(solution)/shard_map/ppermute | solution.py:146
  12.4 7.4 %collective-permute-start.7 = (f32[64,256]{1,0:T(8,128)S(1)}, f32[64,256]{1,0:T(8,128)S(1)}, u32[]{:S(2)}, u32[]{:S(2)}) collective-permute-start(f32[64,256]{1,0:T(8,128)S(1)} %get-tuple-element.28), channel_id=1, source_target_pairs={{0,8},{4,12},{8,0},{12,4},{16,24},{20,28},{24,16},{28,20},{1,9},{5... | collective-permute-start | bytes 196616 | tf_op jit(solution)/shard_map/ppermute | solution.py:146
  14.1 6.0 %collective-permute-start.8 = (f32[64,256]{1,0:T(8,128)S(1)}, f32[64,256]{1,0:T(8,128)S(1)}, u32[]{:S(2)}, u32[]{:S(2)}) collective-permute-start(f32[64,256]{1,0:T(8,128)S(1)} %get-tuple-element.29), channel_id=1, source_target_pairs={{0,16},{4,20},{8,24},{12,28},{16,0},{20,4},{24,8},{28,12},{1,17},{... | collective-permute-start | bytes 196616 | tf_op jit(solution)/shard_map/ppermute | solution.py:146
  15.6 5.8 %collective-permute-start.9 = (f32[64,256]{1,0:T(8,128)S(1)}, f32[64,256]{1,0:T(8,128)S(1)}, u32[]{:S(2)}, u32[]{:S(2)}) collective-permute-start(f32[64,256]{1,0:T(8,128)S(1)} %get-tuple-element.30), channel_id=1, source_target_pairs={{0,24},{4,28},{8,16},{12,20},{16,8},{20,12},{24,0},{28,4},{1,25},{... | collective-permute-start | bytes 196616 | tf_op jit(solution)/shard_map/ppermute | solution.py:146
  16.5 7.6 %collective-permute-start.4 = (f32[64,256]{1,0:T(8,128)S(1)}, f32[64,256]{1,0:T(8,128)S(1)}, u32[]{:S(2)}, u32[]{:S(2)}) collective-permute-start(f32[64,256]{1,0:T(8,128)S(1)} %get-tuple-element.23), channel_id=1, source_target_pairs={{0,8},{4,12},{8,0},{12,4},{16,24},{20,28},{24,16},{28,20},{1,9},{5... | collective-permute-start | bytes 196616 | tf_op jit(solution)/shard_map/ppermute | solution.py:146
  18.2 5.9 %collective-permute-start.5 = (f32[64,256]{1,0:T(8,128)S(1)}, f32[64,256]{1,0:T(8,128)S(1)}, u32[]{:S(2)}, u32[]{:S(2)}) collective-permute-start(f32[64,256]{1,0:T(8,128)S(1)} %get-tuple-element.24), channel_id=1, source_target_pairs={{0,16},{4,20},{8,24},{12,28},{16,0},{20,4},{24,8},{28,12},{1,17},{... | collective-permute-start | bytes 196616 | tf_op jit(solution)/shard_map/ppermute | solution.py:146
  19.8 5.2 %collective-permute-start.6 = (f32[64,256]{1,0:T(8,128)S(1)}, f32[64,256]{1,0:T(8,128)S(1)}, u32[]{:S(2)}, u32[]{:S(2)}) collective-permute-start(f32[64,256]{1,0:T(8,128)S(1)} %get-tuple-element.25), channel_id=1, source_target_pairs={{0,24},{4,28},{8,16},{12,20},{16,8},{20,12},{24,0},{28,4},{1,25},{... | collective-permute-start | bytes 196616 | tf_op jit(solution)/shard_map/ppermute | solution.py:146
  21.5 5.2 %collective-permute-start.10 = (f32[64,256]{1,0:T(8,128)S(1)}, f32[64,256]{1,0:T(8,128)S(1)}, u32[]{:S(2)}, u32[]{:S(2)}) collective-permute-start(f32[64,256]{1,0:T(8,128)S(1)} %add_add_fusion), channel_id=1, source_target_pairs={{0,2},{1,3},{2,0},{3,1},{4,6},{5,7},{6,4},{7,5},{8,10},{9,11},{10,... | collective-permute-start | bytes 196616 | tf_op jit(solution)/shard_map/ppermute | solution.py:146

commit v3 on v2

--- a/solution.py
+++ b/solution.py
@@ -150,16 +150,16 @@
     twin = over("rep", rep, 1, green_samples)
     own_order = turned_order(exchange_index_order, frequency_offset)
     far_order = over("blk", blk, 2, own_order)
-    (own,) = part([(own_order, None, 0)], [green_samples, twin], False)
-    near, own, far_order = lax.optimization_barrier((near, own, far_order))
+    (own,) = part([(own_order, None, 0)], [green_samples], False)
+    near, own, far_order, twin = lax.optimization_barrier((near, own, far_order, twin))
     near_twin = over("rep", rep, 1, near)
-    far, own = part([(far_order, None, 0), (own_order, own, 2)], [green_samples, twin, near], False)
+    far, own = part([(far_order, None, 0), (own_order, own, 1)], [green_samples, twin, near], False)
     (far_parts,) = part([(far_order, far, 0)], [near_twin], True)
     (own_parts,) = part([(own_order, own, 0)], [near_twin], True)
 
     def collect(parts):
         value = parts[0]
-        for step in range(1, rep // 2):
+        for step in range(rep // 2 - 1, 0, -1):
             value = value + over("rep", rep, 2 * step, parts[step])
         return value
 

time: 27.6 us -> 26.5 us (0.960)
  waiting for transfers between devices: 4.66 us -> 3.45 us
    ppermute x11, waiting for transfers between devices: 4.66 us -> 3.45 us  [over(): return lax.ppermute(value, axis, [(i, i ^ flip) for i in range(size)])]
where the time goes in v3:
time: 26.5 us; the launch traced here: 26.3 us
  starting transfers between devices  15.5 us (58%)
  Pallas kernels  4.89 us (18%)
  waiting for transfers between devices  3.45 us (13%)
  local copies, waits for them, and re-layouts  2.34 us (9%)
    ppermute x11, starting transfers between devices, over(): return lax.ppermute(value, axis, [(i, i ^ flip) for i in range(size)])  15.5 us
    ppermute x11, waiting for transfers between devices, over(): return lax.ppermute(value, axis, [(i, i ^ flip) for i in range(size)])  3.45 us
    pallas_call x4, Pallas kernels, partial_tiles(): pl.pallas_call(kernel, out_shape=out_shape, in_specs=[whole] * len(operan...  3.44 us
    unnamed x6, local copies, waits for them, and re-layouts  1.67 us
    pallas_call x1, Pallas kernels, turned_order(): pl.pallas_call(kernel, out_shape=jax.ShapeDtypeStruct(order.shape, order....  1.45 us
    reshape x2, local copies, waits for them, and re-layouts, body(): done = done.reshape(tiles, rows, 2, width)  0.67 us
  transfers between devices with their start and end apart: 11, of which 4 were waited for; matrix products, arithmetic and copies ran while one was open for 0% of the time, Pallas kernels for 16%

profile of v3, /device:TPU:0, one launch (start us, length us, event | category | flops | bytes accessed | tf_op | source)
XLA Modules:
  0.0 26.3 jit_solution(14937033057352115374)
XLA Ops:
  0.0 3.0 %collective-permute-start = (bf16[4,2,128,128]{3,2,1,0:T(8,128)(2,1)}, bf16[4,2,128,128]{3,2,1,0:T(8,128)(2,1)S(1)}, u32[]{:S(2)}, u32[]{:S(2)}) collective-permute-start(bf16[4,2,128,128]{3,2,1,0:T(8,128)(2,1)} %refs_3_.1), channel_id=1, source_target_pairs={{0,1},{1,0},{2,3},{3,2},{4,5},{5,4},{6,7},{7,6},{8,9},{9,8},{10,11... | collective-permute-start | bytes 786440 | tf_op jit(solution)/shard_map/ppermute | solution.py:146
  3.0 0.0 collective-permute-start.2
  3.0 1.4 %shard_map.37.refs_0_.refs_1_ = s32[4,128]{1,0:T(4,128)} custom-call(s32[4,128]{1,0:T(4,128)} %order_ref.1, s32[4]{0:T(128)} %offset_ref.1), custom_call_target="tpu_custom_call" | custom-call | tf_op jit(solution)/shard_map/pallas_call | solution.py:38
  4.5 2.6 %collective-permute-start.1 = (s32[4,128]{1,0:T(4,128)}, s32[4,128]{1,0:T(4,128)S(1)}, u32[]{:S(2)}, u32[]{:S(2)}) collective-permute-start(s32[4,128]{1,0:T(4,128)} %shard_map.37.refs_0_.refs_1_), channel_id=1, source_target_pairs={{0,2},{1,3},{2,0},{3,1},{4,6},{5,7},{6,4},{7,5},{8,10},{9,11},{10,... | collective-permute-start | bytes 6152 | tf_op jit(solution)/shard_map/ppermute | solution.py:146
  7.1 0.0 copy-start
  7.1 0.7 %copy-done = s32[4,128]{1,0:T(4,128)S(1)} copy-done((s32[4,128]{1,0:T(4,128)S(1)}, s32[4,128]{1,0:T(4,128)}, u32[]{:S(2)}) %copy-start) | copy-done | bytes 2072
  7.8 0.9 %copy-done.2 = bf16[4,2,128,128]{3,2,1,0:T(8,128)(2,1)S(1)} copy-done((bf16[4,2,128,128]{3,2,1,0:T(8,128)(2,1)S(1)}, bf16[4,2,128,128]{3,2,1,0:T(8,128)(2,1)}, u32[]{:S(2)}) %copy-start.2) | copy-done | bytes 262168
  8.7 0.6 %shard_map.38.refs_2_ = f32[256,256]{1,0:T(8,128)S(1)} custom-call(s32[4,128]{1,0:T(4,128)S(1)} %copy-done, bf16[4,2,128,128]{3,2,1,0:T(8,128)(2,1)S(1)} %copy-done.2), custom_call_target="tpu_custom_call" | custom-call | flops 268435456 | bytes 262144 | tf_op jit(solution)/shard_map/pallas_call | solution.py:119
  9.3 0.0 collective-permute-done.1.refs_0_
  9.3 0.3 collective-permute-done.refs_5_
  9.6 0.0 collective-permute-done.2.refs_4_
  9.6 0.1 collective-permute-start.3
  9.6 0.0 copy-done.1
  9.6 1.7 %shard_map.39 = (f32[256,256]{1,0:T(8,128)S(1)}, f32[256,256]{1,0:T(8,128)S(1)}) custom-call(s32[4,128]{1,0:T(4,128)S(1)} %collective-permute-done.1.refs_0_, s32[4,128]{1,0:T(4,128)S(1)} %copy-done.1, f32[256,256]{1,0:T(8,128)S(1)} %shard_map.38.refs_2_, bf16[4,2,128,128]{3,2,1,0:T(8,128)(2,1)S(1)} %copy-done.2, ...), custom_call_target="tpu_custom_call" | custom-call | flops 1610612736 | bytes 786432 | tf_op jit(solution)/shard_map/pallas_call | solution.py:119
  11.4 0.0 collective-permute-done.3.refs_2_
  11.4 0.6 %shard_map.41 = (f32[64,256]{1,0:T(8,128)S(1)}, f32[64,256]{1,0:T(8,128)S(1)}, f32[64,256]{1,0:T(8,128)S(1)}, f32[64,256]{1,0:T(8,128)S(1)}) custom-call(s32[4,128]{1,0:T(4,128)S(1)} %collective-permute-done.1.refs_0_, f32[256,256]{1,0:T(8,128)S(1)} %get-tuple-element.28.refs_1_, bf16[4,2,128,128]{3,2,1,0:T(8,128)(2,1)S(1)} %collective-permute-done.3.refs_2_), custom_call_target="tpu_custom_call" | custom-call | flops 268435456 | bytes 262144 | tf_op jit(solution)/shard_map/pallas_call | solution.py:119
  12.0 2.6 %collective-permute-start.7 = (f32[64,256]{1,0:T(8,128)S(1)}, f32[64,256]{1,0:T(8,128)S(1)}, u32[]{:S(2)}, u32[]{:S(2)}) collective-permute-start(f32[64,256]{1,0:T(8,128)S(1)} %get-tuple-element.30), channel_id=1, source_target_pairs={{0,24},{4,28},{8,16},{12,20},{16,8},{20,12},{24,0},{28,4},{1,25},{... | collective-permute-start | bytes 196616 | tf_op jit(solution)/shard_map/ppermute | solution.py:146
  14.6 0.5 %collective-permute-start.8 = (f32[64,256]{1,0:T(8,128)S(1)}, f32[64,256]{1,0:T(8,128)S(1)}, u32[]{:S(2)}, u32[]{:S(2)}) collective-permute-start(f32[64,256]{1,0:T(8,128)S(1)} %get-tuple-element.31), channel_id=1, source_target_pairs={{0,16},{4,20},{8,24},{12,28},{16,0},{20,4},{24,8},{28,12},{1,17},{... | collective-permute-start | bytes 196616 | tf_op jit(solution)/shard_map/ppermute | solution.py:146
  15.1 0.4 %collective-permute-start.9 = (f32[64,256]{1,0:T(8,128)S(1)}, f32[64,256]{1,0:T(8,128)S(1)}, u32[]{:S(2)}, u32[]{:S(2)}) collective-permute-start(f32[64,256]{1,0:T(8,128)S(1)} %get-tuple-element.32), channel_id=1, source_target_pairs={{0,8},{4,12},{8,0},{12,4},{16,24},{20,28},{24,16},{28,20},{1,9},{5... | collective-permute-start | bytes 196616 | tf_op jit(solution)/shard_map/ppermute | solution.py:146
  15.5 0.6 %shard_map.40 = (f32[64,256]{1,0:T(8,128)S(1)}, f32[64,256]{1,0:T(8,128)S(1)}, f32[64,256]{1,0:T(8,128)S(1)}, f32[64,256]{1,0:T(8,128)S(1)}) custom-call(s32[4,128]{1,0:T(4,128)S(1)} %copy-done.1, f32[256,256]{1,0:T(8,128)S(1)} %get-tuple-element.23.refs_1_, bf16[4,2,128,128]{3,2,1,0:T(8,128)(2,1)S(1)} %collective-permute-done.3.refs_2_), custom_call_target="tpu_custom_call" | custom-call | flops 268435456 | bytes 262144 | tf_op jit(solution)/shard_map/pallas_call | solution.py:119
  16.1 2.6 %collective-permute-start.4 = (f32[64,256]{1,0:T(8,128)S(1)}, f32[64,256]{1,0:T(8,128)S(1)}, u32[]{:S(2)}, u32[]{:S(2)}) collective-permute-start(f32[64,256]{1,0:T(8,128)S(1)} %get-tuple-element.25), channel_id=1, source_target_pairs={{0,24},{4,28},{8,16},{12,20},{16,8},{20,12},{24,0},{28,4},{1,25},{... | collective-permute-start | bytes 196616 | tf_op jit(solution)/shard_map/ppermute | solution.py:146
  18.7 0.5 %collective-permute-start.5 = (f32[64,256]{1,0:T(8,128)S(1)}, f32[64,256]{1,0:T(8,128)S(1)}, u32[]{:S(2)}, u32[]{:S(2)}) collective-permute-start(f32[64,256]{1,0:T(8,128)S(1)} %get-tuple-element.26), channel_id=1, source_target_pairs={{0,16},{4,20},{8,24},{12,28},{16,0},{20,4},{24,8},{28,12},{1,17},{... | collective-permute-start | bytes 196616 | tf_op jit(solution)/shard_map/ppermute | solution.py:146
  19.2 0.0 collective-permute-done.7
  19.2 0.4 %collective-permute-start.6 = (f32[64,256]{1,0:T(8,128)S(1)}, f32[64,256]{1,0:T(8,128)S(1)}, u32[]{:S(2)}, u32[]{:S(2)}) collective-permute-start(f32[64,256]{1,0:T(8,128)S(1)} %get-tuple-element.27), channel_id=1, source_target_pairs={{0,8},{4,12},{8,0},{12,4},{16,24},{20,28},{24,16},{28,20},{1,9},{5... | collective-permute-start | bytes 196616 | tf_op jit(solution)/shard_map/ppermute | solution.py:146
  19.7 0.0 collective-permute-done.8
  19.7 0.0 collective-permute-done.9
  19.7 2.8 %collective-permute-start.10 = (f32[64,256]{1,0:T(8,128)S(1)}, f32[64,256]{1,0:T(8,128)S(1)}, u32[]{:S(2)}, u32[]{:S(2)}) collective-permute-start(f32[64,256]{1,0:T(8,128)S(1)} %add_add_fusion), channel_id=1, source_target_pairs={{0,2},{1,3},{2,0},{3,1},{4,6},{5,7},{6,4},{7,5},{8,10},{9,11},{10,... | collective-permute-start | bytes 196616 | tf_op jit(solution)/shard_map/ppermute | solution.py:146
  22.4 0.0 collective-permute-done.4
  22.4 0.6 %collective-permute-done.5 = f32[64,256]{1,0:T(8,128)S(1)} collective-permute-done((f32[64,256]{1,0:T(8,128)S(1)}, f32[64,256]{1,0:T(8,128)S(1)}, u32[]{:S(2)}, u32[]{:S(2)}) %collective-permute-start.5) | collective-permute-done | bytes 65568 | tf_op jit(solution)/shard_map/ppermute | solution.py:146
  23.0 0.5 %collective-permute-done.6 = f32[64,256]{1,0:T(8,128)S(1)} collective-permute-done((f32[64,256]{1,0:T(8,128)S(1)}, f32[64,256]{1,0:T(8,128)S(1)}, u32[]{:S(2)}, u32[]{:S(2)}) %collective-permute-start.6) | collective-permute-done | bytes 65568 | tf_op jit(solution)/shard_map/ppermute | solution.py:146
  23.5 2.1 %collective-permute-done.10 = f32[64,256]{1,0:T(8,128)S(1)} collective-permute-done((f32[64,256]{1,0:T(8,128)S(1)}, f32[64,256]{1,0:T(8,128)S(1)}, u32[]{:S(2)}, u32[]{:S(2)}) %collective-permute-start.10) | collective-permute-done | bytes 65568 | tf_op jit(solution)/shard_map/ppermute | solution.py:146
  25.7 0.6 %copy.6 = f32[4,16,2,128]{3,1,0,2:T(8,128)} copy(f32[4,16,2,128]{3,2,1,0:T(2,128)S(1)} %reshape.3) | data formatting | bytes 131072 | tf_op jit(solution)/shard_map/reshape | solution.py:168
  (5 shorter events, 0.1 us)
Async XLA Ops:
  0.0 9.6 %collective-permute-start = (bf16[4,2,128,128]{3,2,1,0:T(8,128)(2,1)}, bf16[4,2,128,128]{3,2,1,0:T(8,128)(2,1)S(1)}, u32[]{:S(2)}, u32[]{:S(2)}) collective-permute-start(bf16[4,2,128,128]{3,2,1,0:T(8,128)(2,1)} %refs_3_.1), channel_id=1, source_target_pairs={{0,1},{1,0},{2,3},{3,2},{4,5},{5,4},{6,7},{7,6},{8,9},{9,8},{10,11... | collective-permute-start | bytes 786440 | tf_op jit(solution)/shard_map/ppermute | solution.py:146
  3.0 6.6 %collective-permute-start.2 = (bf16[4,2,128,128]{3,2,1,0:T(8,128)(2,1)}, bf16[4,2,128,128]{3,2,1,0:T(8,128)(2,1)S(1)}, u32[]{:S(2)}, u32[]{:S(2)}) collective-permute-start(bf16[4,2,128,128]{3,2,1,0:T(8,128)(2,1)} %refs_3_.1), channel_id=1, source_target_pairs={{0,4},{4,0},{8,12},{12,8},{16,20},{20,16},{24,28},{28,24},{1,5},{5... | collective-permute-start | bytes 786440 | tf_op jit(solution)/shard_map/ppermute | solution.py:146
  4.5 4.8 %collective-permute-start.1 = (s32[4,128]{1,0:T(4,128)}, s32[4,128]{1,0:T(4,128)S(1)}, u32[]{:S(2)}, u32[]{:S(2)}) collective-permute-start(s32[4,128]{1,0:T(4,128)} %shard_map.37.refs_0_.refs_1_), channel_id=1, source_target_pairs={{0,2},{1,3},{2,0},{3,1},{4,6},{5,7},{6,4},{7,5},{8,10},{9,11},{10,... | collective-permute-start | bytes 6152 | tf_op jit(solution)/shard_map/ppermute | solution.py:146
  7.1 0.7 %copy-start = (s32[4,128]{1,0:T(4,128)S(1)}, s32[4,128]{1,0:T(4,128)}, u32[]{:S(2)}) copy-start(s32[4,128]{1,0:T(4,128)} %shard_map.37.refs_0_.refs_1_) | copy-start | bytes 6148
  7.8 0.9 %copy-start.2 = (bf16[4,2,128,128]{3,2,1,0:T(8,128)(2,1)S(1)}, bf16[4,2,128,128]{3,2,1,0:T(8,128)(2,1)}, u32[]{:S(2)}) copy-start(bf16[4,2,128,128]{3,2,1,0:T(8,128)(2,1)} %refs_3_.1) | copy-start | bytes 786436
  8.7 0.9 %copy-start.1 = (s32[4,128]{1,0:T(4,128)S(1)}, s32[4,128]{1,0:T(4,128)}, u32[]{:S(2)}) copy-start(s32[4,128]{1,0:T(4,128)} %shard_map.37.refs_0_.refs_1_) | copy-start | bytes 6148
  9.6 1.8 %collective-permute-start.3 = (bf16[4,2,128,128]{3,2,1,0:T(8,128)(2,1)S(1)}, bf16[4,2,128,128]{3,2,1,0:T(8,128)(2,1)S(1)}, u32[]{:S(2)}, u32[]{:S(2)}) collective-permute-start(bf16[4,2,128,128]{3,2,1,0:T(8,128)(2,1)S(1)} %collective-permute-done.refs_5_), channel_id=1, source_target_pairs={{0,4},{4,0},{8,12},{12,8},{16,20},{20,16},{24,28},{28,24},{1,5},{5... | collective-permute-start | bytes 786440 | tf_op jit(solution)/shard_map/ppermute | solution.py:146
  12.0 7.3 %collective-permute-start.7 = (f32[64,256]{1,0:T(8,128)S(1)}, f32[64,256]{1,0:T(8,128)S(1)}, u32[]{:S(2)}, u32[]{:S(2)}) collective-permute-start(f32[64,256]{1,0:T(8,128)S(1)} %get-tuple-element.30), channel_id=1, source_target_pairs={{0,24},{4,28},{8,16},{12,20},{16,8},{20,12},{24,0},{28,4},{1,25},{... | collective-permute-start | bytes 196616 | tf_op jit(solution)/shard_map/ppermute | solution.py:146
  14.6 5.1 %collective-permute-start.8 = (f32[64,256]{1,0:T(8,128)S(1)}, f32[64,256]{1,0:T(8,128)S(1)}, u32[]{:S(2)}, u32[]{:S(2)}) collective-permute-start(f32[64,256]{1,0:T(8,128)S(1)} %get-tuple-element.31), channel_id=1, source_target_pairs={{0,16},{4,20},{8,24},{12,28},{16,0},{20,4},{24,8},{28,12},{1,17},{... | collective-permute-start | bytes 196616 | tf_op jit(solution)/shard_map/ppermute | solution.py:146
  15.1 4.6 %collective-permute-start.9 = (f32[64,256]{1,0:T(8,128)S(1)}, f32[64,256]{1,0:T(8,128)S(1)}, u32[]{:S(2)}, u32[]{:S(2)}) collective-permute-start(f32[64,256]{1,0:T(8,128)S(1)} %get-tuple-element.32), channel_id=1, source_target_pairs={{0,8},{4,12},{8,0},{12,4},{16,24},{20,28},{24,16},{28,20},{1,9},{5... | collective-permute-start | bytes 196616 | tf_op jit(solution)/shard_map/ppermute | solution.py:146
  16.1 6.3 %collective-permute-start.4 = (f32[64,256]{1,0:T(8,128)S(1)}, f32[64,256]{1,0:T(8,128)S(1)}, u32[]{:S(2)}, u32[]{:S(2)}) collective-permute-start(f32[64,256]{1,0:T(8,128)S(1)} %get-tuple-element.25), channel_id=1, source_target_pairs={{0,24},{4,28},{8,16},{12,20},{16,8},{20,12},{24,0},{28,4},{1,25},{... | collective-permute-start | bytes 196616 | tf_op jit(solution)/shard_map/ppermute | solution.py:146
  18.7 4.3 %collective-permute-start.5 = (f32[64,256]{1,0:T(8,128)S(1)}, f32[64,256]{1,0:T(8,128)S(1)}, u32[]{:S(2)}, u32[]{:S(2)}) collective-permute-start(f32[64,256]{1,0:T(8,128)S(1)} %get-tuple-element.26), channel_id=1, source_target_pairs={{0,16},{4,20},{8,24},{12,28},{16,0},{20,4},{24,8},{28,12},{1,17},{... | collective-permute-start | bytes 196616 | tf_op jit(solution)/shard_map/ppermute | solution.py:146
  19.2 4.3 %collective-permute-start.6 = (f32[64,256]{1,0:T(8,128)S(1)}, f32[64,256]{1,0:T(8,128)S(1)}, u32[]{:S(2)}, u32[]{:S(2)}) collective-permute-start(f32[64,256]{1,0:T(8,128)S(1)} %get-tuple-element.27), channel_id=1, source_target_pairs={{0,8},{4,12},{8,0},{12,4},{16,24},{20,28},{24,16},{28,20},{1,9},{5... | collective-permute-start | bytes 196616 | tf_op jit(solution)/shard_map/ppermute | solution.py:146
  19.7 5.9 %collective-permute-start.10 = (f32[64,256]{1,0:T(8,128)S(1)}, f32[64,256]{1,0:T(8,128)S(1)}, u32[]{:S(2)}, u32[]{:S(2)}) collective-permute-start(f32[64,256]{1,0:T(8,128)S(1)} %add_add_fusion), channel_id=1, source_target_pairs={{0,2},{1,3},{2,0},{3,1},{4,6},{5,7},{6,4},{7,5},{8,10},{9,11},{10,... | collective-permute-start | bytes 196616 | tf_op jit(solution)/shard_map/ppermute | solution.py:146

commit v4 on v3

--- a/solution.py
+++ b/solution.py
@@ -49,6 +49,7 @@
     count = sources[0].shape[0]
     block = owners * rows
     height = tiles * block
+    gathered = tiles - tiles // 4
     step_deep = count * 2 * width
     depth = len(sources) * step_deep
 
@@ -63,17 +64,18 @@
         columns = lax.broadcasted_iota(jnp.int32, (width, width), 0)
         for group, order in enumerate(orders):
             names = order[...]
-            for tile in range(tiles):
+            for tile in range(gathered, tiles):
                 place = (group * tiles + tile) * width
                 hot = jnp.where(columns == names[tile : tile + 1, :], 1.0, 0.0).astype(jnp.bfloat16)
                 table[:, place : place + width] = hot
         for source, sample_ref in enumerate(samples):
             used = [group for group in range(len(groups)) if groups[group][2] <= source]
             for sample in range(count):
+                high = (source * count + sample) * 2 * block
                 for part in range(2):
                     for step in range(owners):
                         owner = (((mine // 2) ^ step) * 2 + mine % 2) * rows
-                        picked[part * block + step * rows : part * block + (step + 1) * rows, :] = sample_ref[
+                        picked[high + part * block + step * rows : high + part * block + (step + 1) * rows, :] = sample_ref[
                             sample, part, pl.ds(pl.multiple_of(owner, rows), rows), :
                         ]
                 real, imag = sample_ref[sample, 0], sample_ref[sample, 1]
@@ -82,18 +84,32 @@
                 right[deep : deep + width, width:] = imag
                 right[deep + width : deep + 2 * width, :width] = -imag
                 right[deep + width : deep + 2 * width, width:] = real
+                wide = [
+                    picked[high + part * block : high + (part + 1) * block, :].astype(jnp.float32) for part in range(2)
+                ]
                 for group in used:
-                    moved = jnp.dot(
-                        picked[...],
-                        table[:, group * tiles * width : (group + 1) * tiles * width],
-                        preferred_element_type=jnp.float32,
-                    ).astype(jnp.bfloat16)
+                    lots = group * tiles
+                    moved = None
+                    if gathered < tiles:
+                        moved = jnp.dot(
+                            picked[high : high + 2 * block, :],
+                            table[:, (lots + gathered) * width : (lots + tiles) * width],
+                            preferred_element_type=jnp.float32,
+                        ).astype(jnp.bfloat16)
                     for tile in range(tiles):
+                        names = jnp.broadcast_to(orders[group][tile : tile + 1, :], (block, width))
                         for part in range(2):
+                            if tile < gathered:
+                                value = jnp.take_along_axis(wide[part], names, axis=1).astype(jnp.bfloat16)
+                            else:
+                                value = moved[
+                                    part * block : (part + 1) * block,
+                                    (tile - gathered) * width : (tile - gathered + 1) * width,
+                                ]
                             left[
                                 group * height + tile * block : group * height + (tile + 1) * block,
                                 deep + part * width : deep + (part + 1) * width,
-                            ] = moved[part * block : (part + 1) * block, tile * width : (tile + 1) * width]
+                            ] = value
         for group, (_, _, first) in enumerate(groups):
             start = first * step_deep
             sums = jnp.dot(
@@ -123,7 +139,7 @@
         out_specs=[whole] * len(out_shape),
         scratch_shapes=[
             pltpu.VMEM((width, len(groups) * tiles * width), jnp.bfloat16),
-            pltpu.VMEM((2 * block, width), jnp.bfloat16),
+            pltpu.VMEM((len(sources) * count * 2 * block, width), jnp.bfloat16),
             pltpu.VMEM((len(groups) * height, depth), jnp.bfloat16),
             pltpu.VMEM((depth, 2 * width), jnp.bfloat16),
             pltpu.VMEM((height, 2 * width), jnp.float32),

time: 26.5 us -> 25.8 us (0.974)
  Pallas kernels: 4.89 us -> 4.11 us
  waiting for transfers between devices: 3.45 us -> 3.72 us
    pallas_call x4, Pallas kernels: 3.44 us -> 2.66 us  [partial_tiles(): pl.pallas_call(kernel, out_shape=out_shape, in_specs=[whole] * len(operan...]
    ppermute x11, waiting for transfers between devices: 3.45 us -> 3.72 us  [over(): return lax.ppermute(value, axis, [(i, i ^ flip) for i in range(size)])]
  transfers between devices with their start and end apart: 11 -> 11, of which waited for: 4 -> 6; matrix products, arithmetic and copies ran while one was open for 0% -> 0% of each run, Pallas kernels for 16% -> 14%
where the time goes in v4:
time: 25.8 us; the launch traced here: 25.6 us
  starting transfers between devices  15.4 us (60%)
  Pallas kernels  4.11 us (16%)
  waiting for transfers between devices  3.72 us (14%)
  local copies, waits for them, and re-layouts  2.34 us (9%)
    ppermute x11, starting transfers between devices, over(): return lax.ppermute(value, axis, [(i, i ^ flip) for i in range(size)])  15.4 us
    ppermute x11, waiting for transfers between devices, over(): return lax.ppermute(value, axis, [(i, i ^ flip) for i in range(size)])  3.72 us
    pallas_call x4, Pallas kernels, partial_tiles(): pl.pallas_call(kernel, out_shape=out_shape, in_specs=[whole] * len(operan...  2.66 us
    unnamed x6, local copies, waits for them, and re-layouts  1.67 us
    pallas_call x1, Pallas kernels, turned_order(): pl.pallas_call(kernel, out_shape=jax.ShapeDtypeStruct(order.shape, order....  1.45 us
    reshape x2, local copies, waits for them, and re-layouts, body(): done = done.reshape(tiles, rows, 2, width)  0.67 us
  transfers between devices with their start and end apart: 11, of which 6 were waited for; matrix products, arithmetic and copies ran while one was open for 0% of the time, Pallas kernels for 14%

profile of v4, /device:TPU:0, one launch (start us, length us, event | category | flops | bytes accessed | tf_op | source)
XLA Modules:
  0.0 25.6 jit_solution(5175731524833387918)
XLA Ops:
  0.0 3.0 %collective-permute-start = (bf16[4,2,128,128]{3,2,1,0:T(8,128)(2,1)}, bf16[4,2,128,128]{3,2,1,0:T(8,128)(2,1)S(1)}, u32[]{:S(2)}, u32[]{:S(2)}) collective-permute-start(bf16[4,2,128,128]{3,2,1,0:T(8,128)(2,1)} %refs_3_.1), channel_id=1, source_target_pairs={{0,1},{1,0},{2,3},{3,2},{4,5},{5,4},{6,7},{7,6},{8,9},{9,8},{10,11... | collective-permute-start | bytes 786440 | tf_op jit(solution)/shard_map/ppermute | solution.py:162
  3.0 0.0 collective-permute-start.2
  3.0 1.4 %shard_map.37.refs_0_.refs_1_ = s32[4,128]{1,0:T(4,128)} custom-call(s32[4,128]{1,0:T(4,128)} %order_ref.1, s32[4]{0:T(128)} %offset_ref.1), custom_call_target="tpu_custom_call" | custom-call | tf_op jit(solution)/shard_map/pallas_call | solution.py:38
  4.5 2.6 %collective-permute-start.1 = (s32[4,128]{1,0:T(4,128)}, s32[4,128]{1,0:T(4,128)S(1)}, u32[]{:S(2)}, u32[]{:S(2)}) collective-permute-start(s32[4,128]{1,0:T(4,128)} %shard_map.37.refs_0_.refs_1_), channel_id=1, source_target_pairs={{0,2},{1,3},{2,0},{3,1},{4,6},{5,7},{6,4},{7,5},{8,10},{9,11},{10,... | collective-permute-start | bytes 6152 | tf_op jit(solution)/shard_map/ppermute | solution.py:162
  7.1 0.0 copy-start
  7.1 0.7 %copy-done = s32[4,128]{1,0:T(4,128)S(1)} copy-done((s32[4,128]{1,0:T(4,128)S(1)}, s32[4,128]{1,0:T(4,128)}, u32[]{:S(2)}) %copy-start) | copy-done | bytes 2072
  7.8 0.9 %copy-done.2 = bf16[4,2,128,128]{3,2,1,0:T(8,128)(2,1)S(1)} copy-done((bf16[4,2,128,128]{3,2,1,0:T(8,128)(2,1)S(1)}, bf16[4,2,128,128]{3,2,1,0:T(8,128)(2,1)}, u32[]{:S(2)}) %copy-start.2) | copy-done | bytes 262168
  8.7 0.5 %shard_map.38.refs_2_ = f32[256,256]{1,0:T(8,128)S(1)} custom-call(s32[4,128]{1,0:T(4,128)S(1)} %copy-done, bf16[4,2,128,128]{3,2,1,0:T(8,128)(2,1)S(1)} %copy-done.2), custom_call_target="tpu_custom_call" | custom-call | flops 268435456 | bytes 262144 | tf_op jit(solution)/shard_map/pallas_call | solution.py:135
  9.2 0.0 collective-permute-done.1.refs_0_
  9.2 0.3 %collective-permute-done.refs_5_ = bf16[4,2,128,128]{3,2,1,0:T(8,128)(2,1)S(1)} collective-permute-done((bf16[4,2,128,128]{3,2,1,0:T(8,128)(2,1)}, bf16[4,2,128,128]{3,2,1,0:T(8,128)(2,1)S(1)}, u32[]{:S(2)}, u32[]{:S(2)}) %collective-permute-start) | collective-permute-done | bytes 262176 | tf_op jit(solution)/shard_map/ppermute | solution.py:162
  9.6 0.0 collective-permute-done.2.refs_4_
  9.6 0.0 collective-permute-start.3
  9.6 0.0 copy-done.1
  9.6 1.2 %shard_map.39 = (f32[256,256]{1,0:T(8,128)S(1)}, f32[256,256]{1,0:T(8,128)S(1)}) custom-call(s32[4,128]{1,0:T(4,128)S(1)} %collective-permute-done.1.refs_0_, s32[4,128]{1,0:T(4,128)S(1)} %copy-done.1, f32[256,256]{1,0:T(8,128)S(1)} %shard_map.38.refs_2_, bf16[4,2,128,128]{3,2,1,0:T(8,128)(2,1)S(1)} %copy-done.2, ...), custom_call_target="tpu_custom_call" | custom-call | flops 1610612736 | bytes 786432 | tf_op jit(solution)/shard_map/pallas_call | solution.py:135
  10.8 0.4 %collective-permute-done.3.refs_2_ = bf16[4,2,128,128]{3,2,1,0:T(8,128)(2,1)S(1)} collective-permute-done((bf16[4,2,128,128]{3,2,1,0:T(8,128)(2,1)S(1)}, bf16[4,2,128,128]{3,2,1,0:T(8,128)(2,1)S(1)}, u32[]{:S(2)}, u32[]{:S(2)}) %collective-permute-start.3) | collective-permute-done | bytes 262176 | tf_op jit(solution)/shard_map/ppermute | solution.py:162
  11.1 0.5 %shard_map.41 = (f32[64,256]{1,0:T(8,128)S(1)}, f32[64,256]{1,0:T(8,128)S(1)}, f32[64,256]{1,0:T(8,128)S(1)}, f32[64,256]{1,0:T(8,128)S(1)}) custom-call(s32[4,128]{1,0:T(4,128)S(1)} %collective-permute-done.1.refs_0_, f32[256,256]{1,0:T(8,128)S(1)} %get-tuple-element.28.refs_1_, bf16[4,2,128,128]{3,2,1,0:T(8,128)(2,1)S(1)} %collective-permute-done.3.refs_2_), custom_call_target="tpu_custom_call" | custom-call | flops 268435456 | bytes 262144 | tf_op jit(solution)/shard_map/pallas_call | solution.py:135
  11.6 2.7 %collective-permute-start.7 = (f32[64,256]{1,0:T(8,128)S(1)}, f32[64,256]{1,0:T(8,128)S(1)}, u32[]{:S(2)}, u32[]{:S(2)}) collective-permute-start(f32[64,256]{1,0:T(8,128)S(1)} %get-tuple-element.30), channel_id=1, source_target_pairs={{0,24},{4,28},{8,16},{12,20},{16,8},{20,12},{24,0},{28,4},{1,25},{... | collective-permute-start | bytes 196616 | tf_op jit(solution)/shard_map/ppermute | solution.py:162
  14.3 0.5 %collective-permute-start.8 = (f32[64,256]{1,0:T(8,128)S(1)}, f32[64,256]{1,0:T(8,128)S(1)}, u32[]{:S(2)}, u32[]{:S(2)}) collective-permute-start(f32[64,256]{1,0:T(8,128)S(1)} %get-tuple-element.31), channel_id=1, source_target_pairs={{0,16},{4,20},{8,24},{12,28},{16,0},{20,4},{24,8},{28,12},{1,17},{... | collective-permute-start | bytes 196616 | tf_op jit(solution)/shard_map/ppermute | solution.py:162
  14.8 0.4 %collective-permute-start.9 = (f32[64,256]{1,0:T(8,128)S(1)}, f32[64,256]{1,0:T(8,128)S(1)}, u32[]{:S(2)}, u32[]{:S(2)}) collective-permute-start(f32[64,256]{1,0:T(8,128)S(1)} %get-tuple-element.32), channel_id=1, source_target_pairs={{0,8},{4,12},{8,0},{12,4},{16,24},{20,28},{24,16},{28,20},{1,9},{5... | collective-permute-start | bytes 196616 | tf_op jit(solution)/shard_map/ppermute | solution.py:162
  15.2 0.5 %shard_map.40 = (f32[64,256]{1,0:T(8,128)S(1)}, f32[64,256]{1,0:T(8,128)S(1)}, f32[64,256]{1,0:T(8,128)S(1)}, f32[64,256]{1,0:T(8,128)S(1)}) custom-call(s32[4,128]{1,0:T(4,128)S(1)} %copy-done.1, f32[256,256]{1,0:T(8,128)S(1)} %get-tuple-element.23.refs_1_, bf16[4,2,128,128]{3,2,1,0:T(8,128)(2,1)S(1)} %collective-permute-done.3.refs_2_), custom_call_target="tpu_custom_call" | custom-call | flops 268435456 | bytes 262144 | tf_op jit(solution)/shard_map/pallas_call | solution.py:135
  15.7 2.7 %collective-permute-start.4 = (f32[64,256]{1,0:T(8,128)S(1)}, f32[64,256]{1,0:T(8,128)S(1)}, u32[]{:S(2)}, u32[]{:S(2)}) collective-permute-start(f32[64,256]{1,0:T(8,128)S(1)} %get-tuple-element.25), channel_id=1, source_target_pairs={{0,24},{4,28},{8,16},{12,20},{16,8},{20,12},{24,0},{28,4},{1,25},{... | collective-permute-start | bytes 196616 | tf_op jit(solution)/shard_map/ppermute | solution.py:162
  18.4 0.5 %collective-permute-start.5 = (f32[64,256]{1,0:T(8,128)S(1)}, f32[64,256]{1,0:T(8,128)S(1)}, u32[]{:S(2)}, u32[]{:S(2)}) collective-permute-start(f32[64,256]{1,0:T(8,128)S(1)} %get-tuple-element.26), channel_id=1, source_target_pairs={{0,16},{4,20},{8,24},{12,28},{16,0},{20,4},{24,8},{28,12},{1,17},{... | collective-permute-start | bytes 196616 | tf_op jit(solution)/shard_map/ppermute | solution.py:162
  18.9 0.0 collective-permute-done.7
  18.9 0.4 %collective-permute-start.6 = (f32[64,256]{1,0:T(8,128)S(1)}, f32[64,256]{1,0:T(8,128)S(1)}, u32[]{:S(2)}, u32[]{:S(2)}) collective-permute-start(f32[64,256]{1,0:T(8,128)S(1)} %get-tuple-element.27), channel_id=1, source_target_pairs={{0,8},{4,12},{8,0},{12,4},{16,24},{20,28},{24,16},{28,20},{1,9},{5... | collective-permute-start | bytes 196616 | tf_op jit(solution)/shard_map/ppermute | solution.py:162
  19.2 0.0 collective-permute-done.8
  19.2 0.2 collective-permute-done.9
  19.5 2.6 %collective-permute-start.10 = (f32[64,256]{1,0:T(8,128)S(1)}, f32[64,256]{1,0:T(8,128)S(1)}, u32[]{:S(2)}, u32[]{:S(2)}) collective-permute-start(f32[64,256]{1,0:T(8,128)S(1)} %add_add_fusion), channel_id=1, source_target_pairs={{0,2},{1,3},{2,0},{3,1},{4,6},{5,7},{6,4},{7,5},{8,10},{9,11},{10,... | collective-permute-start | bytes 196616 | tf_op jit(solution)/shard_map/ppermute | solution.py:162
  22.1 0.0 collective-permute-done.4
  22.1 0.5 %collective-permute-done.5 = f32[64,256]{1,0:T(8,128)S(1)} collective-permute-done((f32[64,256]{1,0:T(8,128)S(1)}, f32[64,256]{1,0:T(8,128)S(1)}, u32[]{:S(2)}, u32[]{:S(2)}) %collective-permute-start.5) | collective-permute-done | bytes 65568 | tf_op jit(solution)/shard_map/ppermute | solution.py:162
  22.6 0.5 %collective-permute-done.6 = f32[64,256]{1,0:T(8,128)S(1)} collective-permute-done((f32[64,256]{1,0:T(8,128)S(1)}, f32[64,256]{1,0:T(8,128)S(1)}, u32[]{:S(2)}, u32[]{:S(2)}) %collective-permute-start.6) | collective-permute-done | bytes 65568 | tf_op jit(solution)/shard_map/ppermute | solution.py:162
  23.1 1.8 %collective-permute-done.10 = f32[64,256]{1,0:T(8,128)S(1)} collective-permute-done((f32[64,256]{1,0:T(8,128)S(1)}, f32[64,256]{1,0:T(8,128)S(1)}, u32[]{:S(2)}, u32[]{:S(2)}) %collective-permute-start.10) | collective-permute-done | bytes 65568 | tf_op jit(solution)/shard_map/ppermute | solution.py:162
  25.0 0.6 %copy.6 = f32[4,16,2,128]{3,1,0,2:T(8,128)} copy(f32[4,16,2,128]{3,2,1,0:T(2,128)S(1)} %reshape.3) | data formatting | bytes 131072 | tf_op jit(solution)/shard_map/reshape | solution.py:184
  (5 shorter events, 0.1 us)
Async XLA Ops:
  0.0 9.6 %collective-permute-start = (bf16[4,2,128,128]{3,2,1,0:T(8,128)(2,1)}, bf16[4,2,128,128]{3,2,1,0:T(8,128)(2,1)S(1)}, u32[]{:S(2)}, u32[]{:S(2)}) collective-permute-start(bf16[4,2,128,128]{3,2,1,0:T(8,128)(2,1)} %refs_3_.1), channel_id=1, source_target_pairs={{0,1},{1,0},{2,3},{3,2},{4,5},{5,4},{6,7},{7,6},{8,9},{9,8},{10,11... | collective-permute-start | bytes 786440 | tf_op jit(solution)/shard_map/ppermute | solution.py:162
  3.0 6.6 %collective-permute-start.2 = (bf16[4,2,128,128]{3,2,1,0:T(8,128)(2,1)}, bf16[4,2,128,128]{3,2,1,0:T(8,128)(2,1)S(1)}, u32[]{:S(2)}, u32[]{:S(2)}) collective-permute-start(bf16[4,2,128,128]{3,2,1,0:T(8,128)(2,1)} %refs_3_.1), channel_id=1, source_target_pairs={{0,4},{4,0},{8,12},{12,8},{16,20},{20,16},{24,28},{28,24},{1,5},{5... | collective-permute-start | bytes 786440 | tf_op jit(solution)/shard_map/ppermute | solution.py:162
  4.5 4.8 %collective-permute-start.1 = (s32[4,128]{1,0:T(4,128)}, s32[4,128]{1,0:T(4,128)S(1)}, u32[]{:S(2)}, u32[]{:S(2)}) collective-permute-start(s32[4,128]{1,0:T(4,128)} %shard_map.37.refs_0_.refs_1_), channel_id=1, source_target_pairs={{0,2},{1,3},{2,0},{3,1},{4,6},{5,7},{6,4},{7,5},{8,10},{9,11},{10,... | collective-permute-start | bytes 6152 | tf_op jit(solution)/shard_map/ppermute | solution.py:162
  7.1 0.7 %copy-start = (s32[4,128]{1,0:T(4,128)S(1)}, s32[4,128]{1,0:T(4,128)}, u32[]{:S(2)}) copy-start(s32[4,128]{1,0:T(4,128)} %shard_map.37.refs_0_.refs_1_) | copy-start | bytes 6148
  7.8 0.9 %copy-start.2 = (bf16[4,2,128,128]{3,2,1,0:T(8,128)(2,1)S(1)}, bf16[4,2,128,128]{3,2,1,0:T(8,128)(2,1)}, u32[]{:S(2)}) copy-start(bf16[4,2,128,128]{3,2,1,0:T(8,128)(2,1)} %refs_3_.1) | copy-start | bytes 786436
  8.7 0.9 %copy-start.1 = (s32[4,128]{1,0:T(4,128)S(1)}, s32[4,128]{1,0:T(4,128)}, u32[]{:S(2)}) copy-start(s32[4,128]{1,0:T(4,128)} %shard_map.37.refs_0_.refs_1_) | copy-start | bytes 6148
  9.6 1.5 %collective-permute-start.3 = (bf16[4,2,128,128]{3,2,1,0:T(8,128)(2,1)S(1)}, bf16[4,2,128,128]{3,2,1,0:T(8,128)(2,1)S(1)}, u32[]{:S(2)}, u32[]{:S(2)}) collective-permute-start(bf16[4,2,128,128]{3,2,1,0:T(8,128)(2,1)S(1)} %collective-permute-done.refs_5_), channel_id=1, source_target_pairs={{0,4},{4,0},{8,12},{12,8},{16,20},{20,16},{24,28},{28,24},{1,5},{5... | collective-permute-start | bytes 786440 | tf_op jit(solution)/shard_map/ppermute | solution.py:162
  11.6 7.2 %collective-permute-start.7 = (f32[64,256]{1,0:T(8,128)S(1)}, f32[64,256]{1,0:T(8,128)S(1)}, u32[]{:S(2)}, u32[]{:S(2)}) collective-permute-start(f32[64,256]{1,0:T(8,128)S(1)} %get-tuple-element.30), channel_id=1, source_target_pairs={{0,24},{4,28},{8,16},{12,20},{16,8},{20,12},{24,0},{28,4},{1,25},{... | collective-permute-start | bytes 196616 | tf_op jit(solution)/shard_map/ppermute | solution.py:162
  14.3 4.9 %collective-permute-start.8 = (f32[64,256]{1,0:T(8,128)S(1)}, f32[64,256]{1,0:T(8,128)S(1)}, u32[]{:S(2)}, u32[]{:S(2)}) collective-permute-start(f32[64,256]{1,0:T(8,128)S(1)} %get-tuple-element.31), channel_id=1, source_target_pairs={{0,16},{4,20},{8,24},{12,28},{16,0},{20,4},{24,8},{28,12},{1,17},{... | collective-permute-start | bytes 196616 | tf_op jit(solution)/shard_map/ppermute | solution.py:162
  14.8 4.6 %collective-permute-start.9 = (f32[64,256]{1,0:T(8,128)S(1)}, f32[64,256]{1,0:T(8,128)S(1)}, u32[]{:S(2)}, u32[]{:S(2)}) collective-permute-start(f32[64,256]{1,0:T(8,128)S(1)} %get-tuple-element.32), channel_id=1, source_target_pairs={{0,8},{4,12},{8,0},{12,4},{16,24},{20,28},{24,16},{28,20},{1,9},{5... | collective-permute-start | bytes 196616 | tf_op jit(solution)/shard_map/ppermute | solution.py:162
  15.7 6.4 %collective-permute-start.4 = (f32[64,256]{1,0:T(8,128)S(1)}, f32[64,256]{1,0:T(8,128)S(1)}, u32[]{:S(2)}, u32[]{:S(2)}) collective-permute-start(f32[64,256]{1,0:T(8,128)S(1)} %get-tuple-element.25), channel_id=1, source_target_pairs={{0,24},{4,28},{8,16},{12,20},{16,8},{20,12},{24,0},{28,4},{1,25},{... | collective-permute-start | bytes 196616 | tf_op jit(solution)/shard_map/ppermute | solution.py:162
  18.4 4.3 %collective-permute-start.5 = (f32[64,256]{1,0:T(8,128)S(1)}, f32[64,256]{1,0:T(8,128)S(1)}, u32[]{:S(2)}, u32[]{:S(2)}) collective-permute-start(f32[64,256]{1,0:T(8,128)S(1)} %get-tuple-element.26), channel_id=1, source_target_pairs={{0,16},{4,20},{8,24},{12,28},{16,0},{20,4},{24,8},{28,12},{1,17},{... | collective-permute-start | bytes 196616 | tf_op jit(solution)/shard_map/ppermute | solution.py:162
  18.9 4.3 %collective-permute-start.6 = (f32[64,256]{1,0:T(8,128)S(1)}, f32[64,256]{1,0:T(8,128)S(1)}, u32[]{:S(2)}, u32[]{:S(2)}) collective-permute-start(f32[64,256]{1,0:T(8,128)S(1)} %get-tuple-element.27), channel_id=1, source_target_pairs={{0,8},{4,12},{8,0},{12,4},{16,24},{20,28},{24,16},{28,20},{1,9},{5... | collective-permute-start | bytes 196616 | tf_op jit(solution)/shard_map/ppermute | solution.py:162
  19.5 5.5 %collective-permute-start.10 = (f32[64,256]{1,0:T(8,128)S(1)}, f32[64,256]{1,0:T(8,128)S(1)}, u32[]{:S(2)}, u32[]{:S(2)}) collective-permute-start(f32[64,256]{1,0:T(8,128)S(1)} %add_add_fusion), channel_id=1, source_target_pairs={{0,2},{1,3},{2,0},{3,1},{4,6},{5,7},{6,4},{7,5},{8,10},{9,11},{10,... | collective-permute-start | bytes 196616 | tf_op jit(solution)/shard_map/ppermute | solution.py:162

commit v5 on v4

--- a/solution.py
+++ b/solution.py
@@ -37,7 +37,7 @@
 
     return pl.pallas_call(
         kernel,
-        out_shape=jax.ShapeDtypeStruct(order.shape, order.dtype),
+        out_shape=pltpu.VMEM(order.shape, order.dtype),
         in_specs=[pl.BlockSpec(memory_space=pltpu.VMEM), pl.BlockSpec(memory_space=pltpu.SMEM)],
         out_specs=pl.BlockSpec(memory_space=pltpu.VMEM),
     )(order, offset)
@@ -59,7 +59,7 @@
         befores = [None if group[1] is None else refs.pop(0) for group in groups]
         samples = [refs.pop(0) for _ in sources]
         outs = [[refs.pop(0) for _ in range(owners if split else 1)] for _ in groups]
-        table, picked, left, right, total = refs
+        table, picked, left, right = refs
         mine = lax.axis_index("rep")
         columns = lax.broadcasted_iota(jnp.int32, (width, width), 0)
         for group, order in enumerate(orders):
@@ -120,11 +120,10 @@
             if not split:
                 outs[group][0][...] = sums
                 continue
-            total[...] = sums
             for step in range(owners):
                 for tile in range(tiles):
                     at = tile * block + step * rows
-                    outs[group][step][tile * rows : (tile + 1) * rows, :] = total[at : at + rows, :]
+                    outs[group][step][tile * rows : (tile + 1) * rows, :] = sums[at : at + rows, :]
 
     if split:
         out_shape = [jax.ShapeDtypeStruct((tiles * rows, 2 * width), jnp.float32)] * (len(groups) * owners)
@@ -142,7 +141,6 @@
             pltpu.VMEM((len(sources) * count * 2 * block, width), jnp.bfloat16),
             pltpu.VMEM((len(groups) * height, depth), jnp.bfloat16),
             pltpu.VMEM((depth, 2 * width), jnp.bfloat16),
-            pltpu.VMEM((height, 2 * width), jnp.float32),
         ],
         compiler_params=pltpu.CompilerParams(vmem_limit_bytes=VMEM_BYTES),
         cost_estimate=pl.CostEstimate(
@@ -162,25 +160,29 @@
         return lax.ppermute(value, axis, [(i, i ^ flip) for i in range(size)])
 
     part = functools.partial(partial_tiles, rep, rows, tiles)
+    flips = range(2, blk, 2)
     near = over("blk", blk, 1, green_samples)
     twin = over("rep", rep, 1, green_samples)
     own_order = turned_order(exchange_index_order, frequency_offset)
-    far_order = over("blk", blk, 2, own_order)
+    far_orders = [over("blk", blk, flip, own_order) for flip in flips]
     (own,) = part([(own_order, None, 0)], [green_samples], False)
-    near, own, far_order, twin = lax.optimization_barrier((near, own, far_order, twin))
+    near, own, far_orders, twin = lax.optimization_barrier((near, own, far_orders, twin))
     near_twin = over("rep", rep, 1, near)
-    far, own = part([(far_order, None, 0), (own_order, own, 1)], [green_samples, twin, near], False)
-    (far_parts,) = part([(far_order, far, 0)], [near_twin], True)
-    (own_parts,) = part([(own_order, own, 0)], [near_twin], True)
-
-    def collect(parts):
+    *fars, own = part(
+        [(order, None, 0) for order in far_orders] + [(own_order, own, 1)], [green_samples, twin, near], False
+    )
+
+    def collect(order, sums):
+        (parts,) = part([(order, sums, 0)], [near_twin], True)
         value = parts[0]
         for step in range(rep // 2 - 1, 0, -1):
             value = value + over("rep", rep, 2 * step, parts[step])
         return value
 
-    far = over("blk", blk, 2, collect(far_parts))
-    done = collect(own_parts) + far
+    others = [over("blk", blk, flip, collect(*each)) for flip, *each in zip(flips, far_orders, fars)]
+    done = collect(own_order, own)
+    for other in others:
+        done = done + other
     done = done.reshape(tiles, rows, 2, width)
     return jnp.transpose(done, (2, 0, 1, 3))
 
@@ -191,7 +193,7 @@
 
     def program(green_samples, exchange_index_order, frequency_offset):
         width = exchange_index_order.shape[1]
-        if blk == 4 and width // rep % 16 == 0:
+        if rep & (rep - 1) == 0 and blk & (blk - 1) == 0 and min(rep, blk) > 1 and width // rep % 16 == 0:
             part = functools.partial(body, rep, blk)
         else:
             part = plain_body

time: 25.8 us -> 25.8 us (level)
  waiting for transfers between devices: 3.72 us -> 5.01 us
  local copies, waits for them, and re-layouts: 2.34 us -> 1.62 us
  Pallas kernels: 4.11 us -> 3.55 us
    ppermute x11, waiting for transfers between devices: 3.72 us -> 5.01 us  [over(): return lax.ppermute(value, axis, [(i, i ^ flip) for i in range(size)])]
    unnamed x6 -> x2, local copies, waits for them, and re-layouts: 1.67 us -> 0.95 us
    pallas_call x1, Pallas kernels: 1.45 us -> 0.87 us  [turned_order(): pl.pallas_call(kernel, out_shape=pltpu.VMEM(order.shape, order.dtype), in...]
  transfers between devices with their start and end apart: 11 -> 11, of which waited for: 6 -> 7; matrix products, arithmetic and copies ran while one was open for 0% -> 0% of each run, Pallas kernels for 14% -> 12%
where the time goes in v5:
time: 25.8 us; the launch traced here: 25.6 us
  starting transfers between devices  15.4 us (60%)
  waiting for transfers between devices  5.01 us (19%)
  Pallas kernels  3.55 us (14%)
  local copies, waits for them, and re-layouts  1.62 us (6%)
    ppermute x11, starting transfers between devices, over(): return lax.ppermute(value, axis, [(i, i ^ flip) for i in range(size)])  15.4 us
    ppermute x11, waiting for transfers between devices, over(): return lax.ppermute(value, axis, [(i, i ^ flip) for i in range(size)])  5.01 us
    pallas_call x4, Pallas kernels, partial_tiles(): pl.pallas_call(kernel, out_shape=out_shape, in_specs=[whole] * len(operan...  2.68 us
    unnamed x2, local copies, waits for them, and re-layouts  0.95 us
    pallas_call x1, Pallas kernels, turned_order(): pl.pallas_call(kernel, out_shape=pltpu.VMEM(order.shape, order.dtype), in...  0.87 us
    reshape x2, local copies, waits for them, and re-layouts, body(): done = done.reshape(tiles, rows, 2, width)  0.67 us
  transfers between devices with their start and end apart: 11, of which 7 were waited for; matrix products, arithmetic and copies ran while one was open for 0% of the time, Pallas kernels for 12%

profile of v5, /device:TPU:0, one launch (start us, length us, event | category | flops | bytes accessed | tf_op | source)
XLA Modules:
  0.0 25.6 jit_solution(16739015259362601916)
XLA Ops:
  0.0 3.0 %collective-permute-start = (bf16[4,2,128,128]{3,2,1,0:T(8,128)(2,1)}, bf16[4,2,128,128]{3,2,1,0:T(8,128)(2,1)S(1)}, u32[]{:S(2)}, u32[]{:S(2)}) collective-permute-start(bf16[4,2,128,128]{3,2,1,0:T(8,128)(2,1)} %refs_3_.1), channel_id=1, source_target_pairs={{0,1},{1,0},{2,3},{3,2},{4,5},{5,4},{6,7},{7,6},{8,9},{9,8},{10,11... | collective-permute-start | bytes 786440 | tf_op jit(solution)/shard_map/ppermute | solution.py:160
  3.0 0.0 collective-permute-start.2
  3.0 0.9 %shard_map.37.refs_0_.refs_1_ = s32[4,128]{1,0:T(4,128)S(1)} custom-call(s32[4,128]{1,0:T(4,128)} %order_ref.1, s32[4]{0:T(128)} %offset_ref.1), custom_call_target="tpu_custom_call" | custom-call | tf_op jit(solution)/shard_map/pallas_call | solution.py:38
  3.9 2.6 %collective-permute-start.1 = (s32[4,128]{1,0:T(4,128)S(1)}, s32[4,128]{1,0:T(4,128)S(1)}, u32[]{:S(2)}, u32[]{:S(2)}) collective-permute-start(s32[4,128]{1,0:T(4,128)S(1)} %shard_map.37.refs_0_.refs_1_), channel_id=1, source_target_pairs={{0,2},{1,3},{2,0},{3,1},{4,6},{5,7},{6,4},{7,5},{8,10},{9,11},{10,... | collective-permute-start | bytes 6152 | tf_op jit(solution)/shard_map/ppermute | solution.py:160
  6.5 0.0 copy-start
  6.5 0.9 %copy-done = bf16[4,2,128,128]{3,2,1,0:T(8,128)(2,1)S(1)} copy-done((bf16[4,2,128,128]{3,2,1,0:T(8,128)(2,1)S(1)}, bf16[4,2,128,128]{3,2,1,0:T(8,128)(2,1)}, u32[]{:S(2)}) %copy-start) | copy-done | bytes 262168
  7.4 0.5 %shard_map.38.refs_2_ = f32[256,256]{1,0:T(8,128)S(1)} custom-call(s32[4,128]{1,0:T(4,128)S(1)} %shard_map.37.refs_0_.refs_1_, bf16[4,2,128,128]{3,2,1,0:T(8,128)(2,1)S(1)} %copy-done), custom_call_target="tpu_custom_call" | custom-call | flops 268435456 | bytes 262144 | tf_op jit(solution)/shard_map/pallas_call | solution.py:134
  7.9 1.0 %collective-permute-done.1.refs_0_ = s32[4,128]{1,0:T(4,128)S(1)} collective-permute-done((s32[4,128]{1,0:T(4,128)S(1)}, s32[4,128]{1,0:T(4,128)S(1)}, u32[]{:S(2)}, u32[]{:S(2)}) %collective-permute-start.1) | collective-permute-done | bytes 2080 | tf_op jit(solution)/shard_map/ppermute | solution.py:160
  8.9 0.7 %collective-permute-done.refs_5_ = bf16[4,2,128,128]{3,2,1,0:T(8,128)(2,1)S(1)} collective-permute-done((bf16[4,2,128,128]{3,2,1,0:T(8,128)(2,1)}, bf16[4,2,128,128]{3,2,1,0:T(8,128)(2,1)S(1)}, u32[]{:S(2)}, u32[]{:S(2)}) %collective-permute-start) | collective-permute-done | bytes 262176 | tf_op jit(solution)/shard_map/ppermute | solution.py:160
  9.6 0.0 collective-permute-done.2.refs_4_
  9.6 0.0 collective-permute-start.3
  9.6 1.2 %shard_map.39 = (f32[256,256]{1,0:T(8,128)S(1)}, f32[256,256]{1,0:T(8,128)S(1)}) custom-call(s32[4,128]{1,0:T(4,128)S(1)} %collective-permute-done.1.refs_0_, s32[4,128]{1,0:T(4,128)S(1)} %shard_map.37.refs_0_.refs_1_, f32[256,256]{1,0:T(8,128)S(1)} %shard_map.38.refs_2_, bf16[4,2,128,128]{3,2,1,0:T(8,128)(2,1)S(1)} %copy-done, ...), custom_call_target="tpu_custom_call" | custom-call | flops 1610612736 | bytes 786432 | tf_op jit(solution)/shard_map/pallas_call | solution.py:134
  10.8 0.3 %collective-permute-done.3.refs_2_ = bf16[4,2,128,128]{3,2,1,0:T(8,128)(2,1)S(1)} collective-permute-done((bf16[4,2,128,128]{3,2,1,0:T(8,128)(2,1)S(1)}, bf16[4,2,128,128]{3,2,1,0:T(8,128)(2,1)S(1)}, u32[]{:S(2)}, u32[]{:S(2)}) %collective-permute-start.3) | collective-permute-done | bytes 262176 | tf_op jit(solution)/shard_map/ppermute | solution.py:160
  11.1 0.5 %shard_map.41 = (f32[64,256]{1,0:T(8,128)S(1)}, f32[64,256]{1,0:T(8,128)S(1)}, f32[64,256]{1,0:T(8,128)S(1)}, f32[64,256]{1,0:T(8,128)S(1)}) custom-call(s32[4,128]{1,0:T(4,128)S(1)} %collective-permute-done.1.refs_0_, f32[256,256]{1,0:T(8,128)S(1)} %get-tuple-element.28.refs_1_, bf16[4,2,128,128]{3,2,1,0:T(8,128)(2,1)S(1)} %collective-permute-done.3.refs_2_), custom_call_target="tpu_custom_call" | custom-call | flops 268435456 | bytes 262144 | tf_op jit(solution)/shard_map/pallas_call | solution.py:134
  11.6 2.7 %collective-permute-start.7 = (f32[64,256]{1,0:T(8,128)S(1)}, f32[64,256]{1,0:T(8,128)S(1)}, u32[]{:S(2)}, u32[]{:S(2)}) collective-permute-start(f32[64,256]{1,0:T(8,128)S(1)} %get-tuple-element.30), channel_id=1, source_target_pairs={{0,24},{4,28},{8,16},{12,20},{16,8},{20,12},{24,0},{28,4},{1,25},{... | collective-permute-start | bytes 196616 | tf_op jit(solution)/shard_map/ppermute | solution.py:160
  14.3 0.5 %collective-permute-start.8 = (f32[64,256]{1,0:T(8,128)S(1)}, f32[64,256]{1,0:T(8,128)S(1)}, u32[]{:S(2)}, u32[]{:S(2)}) collective-permute-start(f32[64,256]{1,0:T(8,128)S(1)} %get-tuple-element.31), channel_id=1, source_target_pairs={{0,16},{4,20},{8,24},{12,28},{16,0},{20,4},{24,8},{28,12},{1,17},{... | collective-permute-start | bytes 196616 | tf_op jit(solution)/shard_map/ppermute | solution.py:160
  14.8 0.4 %collective-permute-start.9 = (f32[64,256]{1,0:T(8,128)S(1)}, f32[64,256]{1,0:T(8,128)S(1)}, u32[]{:S(2)}, u32[]{:S(2)}) collective-permute-start(f32[64,256]{1,0:T(8,128)S(1)} %get-tuple-element.32), channel_id=1, source_target_pairs={{0,8},{4,12},{8,0},{12,4},{16,24},{20,28},{24,16},{28,20},{1,9},{5... | collective-permute-start | bytes 196616 | tf_op jit(solution)/shard_map/ppermute | solution.py:160
  15.2 0.5 %shard_map.40 = (f32[64,256]{1,0:T(8,128)S(1)}, f32[64,256]{1,0:T(8,128)S(1)}, f32[64,256]{1,0:T(8,128)S(1)}, f32[64,256]{1,0:T(8,128)S(1)}) custom-call(s32[4,128]{1,0:T(4,128)S(1)} %shard_map.37.refs_0_.refs_1_, f32[256,256]{1,0:T(8,128)S(1)} %get-tuple-element.23.refs_1_, bf16[4,2,128,128]{3,2,1,0:T(8,128)(2,1)S(1)} %collective-permute-done.3.refs_2_), custom_call_target="tpu_custom_call" | custom-call | flops 268435456 | bytes 262144 | tf_op jit(solution)/shard_map/pallas_call | solution.py:134
  15.7 2.7 %collective-permute-start.4 = (f32[64,256]{1,0:T(8,128)S(1)}, f32[64,256]{1,0:T(8,128)S(1)}, u32[]{:S(2)}, u32[]{:S(2)}) collective-permute-start(f32[64,256]{1,0:T(8,128)S(1)} %get-tuple-element.25), channel_id=1, source_target_pairs={{0,24},{4,28},{8,16},{12,20},{16,8},{20,12},{24,0},{28,4},{1,25},{... | collective-permute-start | bytes 196616 | tf_op jit(solution)/shard_map/ppermute | solution.py:160
  18.4 0.5 %collective-permute-start.5 = (f32[64,256]{1,0:T(8,128)S(1)}, f32[64,256]{1,0:T(8,128)S(1)}, u32[]{:S(2)}, u32[]{:S(2)}) collective-permute-start(f32[64,256]{1,0:T(8,128)S(1)} %get-tuple-element.26), channel_id=1, source_target_pairs={{0,16},{4,20},{8,24},{12,28},{16,0},{20,4},{24,8},{28,12},{1,17},{... | collective-permute-start | bytes 196616 | tf_op jit(solution)/shard_map/ppermute | solution.py:160
  18.9 0.0 collective-permute-done.7
  18.9 0.4 %collective-permute-start.6 = (f32[64,256]{1,0:T(8,128)S(1)}, f32[64,256]{1,0:T(8,128)S(1)}, u32[]{:S(2)}, u32[]{:S(2)}) collective-permute-start(f32[64,256]{1,0:T(8,128)S(1)} %get-tuple-element.27), channel_id=1, source_target_pairs={{0,8},{4,12},{8,0},{12,4},{16,24},{20,28},{24,16},{28,20},{1,9},{5... | collective-permute-start | bytes 196616 | tf_op jit(solution)/shard_map/ppermute | solution.py:160
  19.2 0.0 collective-permute-done.8
  19.2 0.2 collective-permute-done.9
  19.5 2.6 %collective-permute-start.10 = (f32[64,256]{1,0:T(8,128)S(1)}, f32[64,256]{1,0:T(8,128)S(1)}, u32[]{:S(2)}, u32[]{:S(2)}) collective-permute-start(f32[64,256]{1,0:T(8,128)S(1)} %add_add_fusion), channel_id=1, source_target_pairs={{0,2},{1,3},{2,0},{3,1},{4,6},{5,7},{6,4},{7,5},{8,10},{9,11},{10,... | collective-permute-start | bytes 196616 | tf_op jit(solution)/shard_map/ppermute | solution.py:160
  22.1 0.0 collective-permute-done.4
  22.1 0.5 %collective-permute-done.5 = f32[64,256]{1,0:T(8,128)S(1)} collective-permute-done((f32[64,256]{1,0:T(8,128)S(1)}, f32[64,256]{1,0:T(8,128)S(1)}, u32[]{:S(2)}, u32[]{:S(2)}) %collective-permute-start.5) | collective-permute-done | bytes 65568 | tf_op jit(solution)/shard_map/ppermute | solution.py:160
  22.6 0.5 %collective-permute-done.6 = f32[64,256]{1,0:T(8,128)S(1)} collective-permute-done((f32[64,256]{1,0:T(8,128)S(1)}, f32[64,256]{1,0:T(8,128)S(1)}, u32[]{:S(2)}, u32[]{:S(2)}) %collective-permute-start.6) | collective-permute-done | bytes 65568 | tf_op jit(solution)/shard_map/ppermute | solution.py:160
  23.1 1.8 %collective-permute-done.10 = f32[64,256]{1,0:T(8,128)S(1)} collective-permute-done((f32[64,256]{1,0:T(8,128)S(1)}, f32[64,256]{1,0:T(8,128)S(1)}, u32[]{:S(2)}, u32[]{:S(2)}) %collective-permute-start.10) | collective-permute-done | bytes 65568 | tf_op jit(solution)/shard_map/ppermute | solution.py:160
  25.0 0.6 %copy.6 = f32[4,16,2,128]{3,1,0,2:T(8,128)} copy(f32[4,16,2,128]{3,2,1,0:T(2,128)S(1)} %reshape.3) | data formatting | bytes 131072 | tf_op jit(solution)/shard_map/reshape | solution.py:186
  (3 shorter events, 0.1 us)
Async XLA Ops:
  0.0 9.6 %collective-permute-start = (bf16[4,2,128,128]{3,2,1,0:T(8,128)(2,1)}, bf16[4,2,128,128]{3,2,1,0:T(8,128)(2,1)S(1)}, u32[]{:S(2)}, u32[]{:S(2)}) collective-permute-start(bf16[4,2,128,128]{3,2,1,0:T(8,128)(2,1)} %refs_3_.1), channel_id=1, source_target_pairs={{0,1},{1,0},{2,3},{3,2},{4,5},{5,4},{6,7},{7,6},{8,9},{9,8},{10,11... | collective-permute-start | bytes 786440 | tf_op jit(solution)/shard_map/ppermute | solution.py:160
  3.0 6.6 %collective-permute-start.2 = (bf16[4,2,128,128]{3,2,1,0:T(8,128)(2,1)}, bf16[4,2,128,128]{3,2,1,0:T(8,128)(2,1)S(1)}, u32[]{:S(2)}, u32[]{:S(2)}) collective-permute-start(bf16[4,2,128,128]{3,2,1,0:T(8,128)(2,1)} %refs_3_.1), channel_id=1, source_target_pairs={{0,4},{4,0},{8,12},{12,8},{16,20},{20,16},{24,28},{28,24},{1,5},{5... | collective-permute-start | bytes 786440 | tf_op jit(solution)/shard_map/ppermute | solution.py:160
  3.9 5.0 %collective-permute-start.1 = (s32[4,128]{1,0:T(4,128)S(1)}, s32[4,128]{1,0:T(4,128)S(1)}, u32[]{:S(2)}, u32[]{:S(2)}) collective-permute-start(s32[4,128]{1,0:T(4,128)S(1)} %shard_map.37.refs_0_.refs_1_), channel_id=1, source_target_pairs={{0,2},{1,3},{2,0},{3,1},{4,6},{5,7},{6,4},{7,5},{8,10},{9,11},{10,... | collective-permute-start | bytes 6152 | tf_op jit(solution)/shard_map/ppermute | solution.py:160
  6.5 0.9 %copy-start = (bf16[4,2,128,128]{3,2,1,0:T(8,128)(2,1)S(1)}, bf16[4,2,128,128]{3,2,1,0:T(8,128)(2,1)}, u32[]{:S(2)}) copy-start(bf16[4,2,128,128]{3,2,1,0:T(8,128)(2,1)} %refs_3_.1) | copy-start | bytes 786436
  9.6 1.5 %collective-permute-start.3 = (bf16[4,2,128,128]{3,2,1,0:T(8,128)(2,1)S(1)}, bf16[4,2,128,128]{3,2,1,0:T(8,128)(2,1)S(1)}, u32[]{:S(2)}, u32[]{:S(2)}) collective-permute-start(bf16[4,2,128,128]{3,2,1,0:T(8,128)(2,1)S(1)} %collective-permute-done.refs_5_), channel_id=1, source_target_pairs={{0,4},{4,0},{8,12},{12,8},{16,20},{20,16},{24,28},{28,24},{1,5},{5... | collective-permute-start | bytes 786440 | tf_op jit(solution)/shard_map/ppermute | solution.py:160
  11.6 7.2 %collective-permute-start.7 = (f32[64,256]{1,0:T(8,128)S(1)}, f32[64,256]{1,0:T(8,128)S(1)}, u32[]{:S(2)}, u32[]{:S(2)}) collective-permute-start(f32[64,256]{1,0:T(8,128)S(1)} %get-tuple-element.30), channel_id=1, source_target_pairs={{0,24},{4,28},{8,16},{12,20},{16,8},{20,12},{24,0},{28,4},{1,25},{... | collective-permute-start | bytes 196616 | tf_op jit(solution)/shard_map/ppermute | solution.py:160
  14.3 4.9 %collective-permute-start.8 = (f32[64,256]{1,0:T(8,128)S(1)}, f32[64,256]{1,0:T(8,128)S(1)}, u32[]{:S(2)}, u32[]{:S(2)}) collective-permute-start(f32[64,256]{1,0:T(8,128)S(1)} %get-tuple-element.31), channel_id=1, source_target_pairs={{0,16},{4,20},{8,24},{12,28},{16,0},{20,4},{24,8},{28,12},{1,17},{... | collective-permute-start | bytes 196616 | tf_op jit(solution)/shard_map/ppermute | solution.py:160
  14.8 4.6 %collective-permute-start.9 = (f32[64,256]{1,0:T(8,128)S(1)}, f32[64,256]{1,0:T(8,128)S(1)}, u32[]{:S(2)}, u32[]{:S(2)}) collective-permute-start(f32[64,256]{1,0:T(8,128)S(1)} %get-tuple-element.32), channel_id=1, source_target_pairs={{0,8},{4,12},{8,0},{12,4},{16,24},{20,28},{24,16},{28,20},{1,9},{5... | collective-permute-start | bytes 196616 | tf_op jit(solution)/shard_map/ppermute | solution.py:160
  15.7 6.4 %collective-permute-start.4 = (f32[64,256]{1,0:T(8,128)S(1)}, f32[64,256]{1,0:T(8,128)S(1)}, u32[]{:S(2)}, u32[]{:S(2)}) collective-permute-start(f32[64,256]{1,0:T(8,128)S(1)} %get-tuple-element.25), channel_id=1, source_target_pairs={{0,24},{4,28},{8,16},{12,20},{16,8},{20,12},{24,0},{28,4},{1,25},{... | collective-permute-start | bytes 196616 | tf_op jit(solution)/shard_map/ppermute | solution.py:160
  18.4 4.3 %collective-permute-start.5 = (f32[64,256]{1,0:T(8,128)S(1)}, f32[64,256]{1,0:T(8,128)S(1)}, u32[]{:S(2)}, u32[]{:S(2)}) collective-permute-start(f32[64,256]{1,0:T(8,128)S(1)} %get-tuple-element.26), channel_id=1, source_target_pairs={{0,16},{4,20},{8,24},{12,28},{16,0},{20,4},{24,8},{28,12},{1,17},{... | collective-permute-start | bytes 196616 | tf_op jit(solution)/shard_map/ppermute | solution.py:160
  18.9 4.3 %collective-permute-start.6 = (f32[64,256]{1,0:T(8,128)S(1)}, f32[64,256]{1,0:T(8,128)S(1)}, u32[]{:S(2)}, u32[]{:S(2)}) collective-permute-start(f32[64,256]{1,0:T(8,128)S(1)} %get-tuple-element.27), channel_id=1, source_target_pairs={{0,8},{4,12},{8,0},{12,4},{16,24},{20,28},{24,16},{28,20},{1,9},{5... | collective-permute-start | bytes 196616 | tf_op jit(solution)/shard_map/ppermute | solution.py:160
  19.5 5.5 %collective-permute-start.10 = (f32[64,256]{1,0:T(8,128)S(1)}, f32[64,256]{1,0:T(8,128)S(1)}, u32[]{:S(2)}, u32[]{:S(2)}) collective-permute-start(f32[64,256]{1,0:T(8,128)S(1)} %add_add_fusion), channel_id=1, source_target_pairs={{0,2},{1,3},{2,0},{3,1},{4,6},{5,7},{6,4},{7,5},{8,10},{9,11},{10,... | collective-permute-start | bytes 196616 | tf_op jit(solution)/shard_map/ppermute | solution.py:160

commit v6 on v5

--- a/solution.py
+++ b/solution.py
@@ -41,6 +41,12 @@
         in_specs=[pl.BlockSpec(memory_space=pltpu.VMEM), pl.BlockSpec(memory_space=pltpu.SMEM)],
         out_specs=pl.BlockSpec(memory_space=pltpu.VMEM),
     )(order, offset)
+
+
+def owner_of(rep, mine, step):
+    chip, core = mine // 2, mine % 2
+    turned = step % (rep // 2 - 1) + 1 if step else 0
+    return (chip ^ (step + core * (turned - step))) * 2 + core
 
 
 def partial_tiles(rep, rows, tiles, groups, sources, split):
@@ -74,7 +80,7 @@
                 high = (source * count + sample) * 2 * block
                 for part in range(2):
                     for step in range(owners):
-                        owner = (((mine // 2) ^ step) * 2 + mine % 2) * rows
+                        owner = owner_of(rep, mine, step) * rows
                         picked[high + part * block + step * rows : high + part * block + (step + 1) * rows, :] = sample_ref[
                             sample, part, pl.ds(pl.multiple_of(owner, rows), rows), :
                         ]
@@ -176,7 +182,7 @@
         (parts,) = part([(order, sums, 0)], [near_twin], True)
         value = parts[0]
         for step in range(rep // 2 - 1, 0, -1):
-            value = value + over("rep", rep, 2 * step, parts[step])
+            value = value + lax.ppermute(parts[step], "rep", [(i, owner_of(rep, i, step)) for i in range(rep)])
         return value
 
     others = [over("blk", blk, flip, collect(*each)) for flip, *each in zip(flips, far_orders, fars)]

time: 25.8 us -> 25.4 us (0.984)
  waiting for transfers between devices: 5.01 us -> 4.41 us
    ppermute x0 -> x6, starting transfers between devices: none -> 7.11 us  [collect(): lax.ppermute(parts[step], 'rep', [(i, owner_of(rep, i, step)) for i in ra...]
    ppermute x11 -> x5, starting transfers between devices: 15.4 us -> 8.42 us  [over(): return lax.ppermute(value, axis, [(i, i ^ flip) for i in range(size)])]
    ppermute x11 -> x5, waiting for transfers between devices: 5.01 us -> 3.33 us  [over(): return lax.ppermute(value, axis, [(i, i ^ flip) for i in range(size)])]
    ppermute x0 -> x6, waiting for transfers between devices: none -> 1.07 us  [collect(): lax.ppermute(parts[step], 'rep', [(i, owner_of(rep, i, step)) for i in ra...]
  transfers between devices with their start and end apart: 11 -> 11, of which waited for: 7 -> 6; matrix products, arithmetic and copies ran while one was open for 0% -> 0% of each run, Pallas kernels for 12% -> 12%
where the time goes in v6:
time: 25.4 us; the launch traced here: 25.2 us
  starting transfers between devices  15.5 us (61%)
  waiting for transfers between devices  4.41 us (17%)
  Pallas kernels  3.58 us (14%)
  local copies, waits for them, and re-layouts  1.62 us (6%)
    ppermute x5, starting transfers between devices, over(): return lax.ppermute(value, axis, [(i, i ^ flip) for i in range(size)])  8.42 us
    ppermute x6, starting transfers between devices, collect(): lax.ppermute(parts[step], 'rep', [(i, owner_of(rep, i, step)) for i in ra...  7.11 us
    ppermute x5, waiting for transfers between devices, over(): return lax.ppermute(value, axis, [(i, i ^ flip) for i in range(size)])  3.33 us
    pallas_call x4, Pallas kernels, partial_tiles(): pl.pallas_call(kernel, out_shape=out_shape, in_specs=[whole] * len(operan...  2.71 us
    ppermute x6, waiting for transfers between devices, collect(): lax.ppermute(parts[step], 'rep', [(i, owner_of(rep, i, step)) for i in ra...  1.07 us
    unnamed x2, local copies, waits for them, and re-layouts  0.95 us
    pallas_call x1, Pallas kernels, turned_order(): pl.pallas_call(kernel, out_shape=pltpu.VMEM(order.shape, order.dtype), in...  0.87 us
    reshape x2, local copies, waits for them, and re-layouts, body(): done = done.reshape(tiles, rows, 2, width)  0.67 us
  transfers between devices with their start and end apart: 11, of which 6 were waited for; matrix products, arithmetic and copies ran while one was open for 0% of the time, Pallas kernels for 12%

profile of v6, /device:TPU:0, one launch (start us, length us, event | category | flops | bytes accessed | tf_op | source)
XLA Modules:
  0.0 25.2 jit_solution(447315241543622563)
XLA Ops:
  0.0 3.0 %collective-permute-start = (bf16[4,2,128,128]{3,2,1,0:T(8,128)(2,1)}, bf16[4,2,128,128]{3,2,1,0:T(8,128)(2,1)S(1)}, u32[]{:S(2)}, u32[]{:S(2)}) collective-permute-start(bf16[4,2,128,128]{3,2,1,0:T(8,128)(2,1)} %refs_3_.1), channel_id=1, source_target_pairs={{0,1},{1,0},{2,3},{3,2},{4,5},{5,4},{6,7},{7,6},{8,9},{9,8},{10,11... | collective-permute-start | bytes 786440 | tf_op jit(solution)/shard_map/ppermute | solution.py:166
  3.0 0.0 collective-permute-start.2
  3.0 0.9 %shard_map.37.refs_0_.refs_1_ = s32[4,128]{1,0:T(4,128)S(1)} custom-call(s32[4,128]{1,0:T(4,128)} %order_ref.1, s32[4]{0:T(128)} %offset_ref.1), custom_call_target="tpu_custom_call" | custom-call | tf_op jit(solution)/shard_map/pallas_call | solution.py:38
  3.9 2.6 %collective-permute-start.1 = (s32[4,128]{1,0:T(4,128)S(1)}, s32[4,128]{1,0:T(4,128)S(1)}, u32[]{:S(2)}, u32[]{:S(2)}) collective-permute-start(s32[4,128]{1,0:T(4,128)S(1)} %shard_map.37.refs_0_.refs_1_), channel_id=1, source_target_pairs={{0,2},{1,3},{2,0},{3,1},{4,6},{5,7},{6,4},{7,5},{8,10},{9,11},{10,... | collective-permute-start | bytes 6152 | tf_op jit(solution)/shard_map/ppermute | solution.py:166
  6.5 0.0 copy-start
  6.5 0.9 %copy-done = bf16[4,2,128,128]{3,2,1,0:T(8,128)(2,1)S(1)} copy-done((bf16[4,2,128,128]{3,2,1,0:T(8,128)(2,1)S(1)}, bf16[4,2,128,128]{3,2,1,0:T(8,128)(2,1)}, u32[]{:S(2)}) %copy-start) | copy-done | bytes 262168
  7.4 0.5 %shard_map.38.refs_2_ = f32[256,256]{1,0:T(8,128)S(1)} custom-call(s32[4,128]{1,0:T(4,128)S(1)} %shard_map.37.refs_0_.refs_1_, bf16[4,2,128,128]{3,2,1,0:T(8,128)(2,1)S(1)} %copy-done), custom_call_target="tpu_custom_call" | custom-call | flops 268435456 | bytes 262144 | tf_op jit(solution)/shard_map/pallas_call | solution.py:140
  8.0 1.0 %collective-permute-done.1.refs_0_ = s32[4,128]{1,0:T(4,128)S(1)} collective-permute-done((s32[4,128]{1,0:T(4,128)S(1)}, s32[4,128]{1,0:T(4,128)S(1)}, u32[]{:S(2)}, u32[]{:S(2)}) %collective-permute-start.1) | collective-permute-done | bytes 2080 | tf_op jit(solution)/shard_map/ppermute | solution.py:166
  8.9 0.7 %collective-permute-done.refs_5_ = bf16[4,2,128,128]{3,2,1,0:T(8,128)(2,1)S(1)} collective-permute-done((bf16[4,2,128,128]{3,2,1,0:T(8,128)(2,1)}, bf16[4,2,128,128]{3,2,1,0:T(8,128)(2,1)S(1)}, u32[]{:S(2)}, u32[]{:S(2)}) %collective-permute-start) | collective-permute-done | bytes 262176 | tf_op jit(solution)/shard_map/ppermute | solution.py:166
  9.6 0.0 collective-permute-done.2.refs_4_
  9.6 0.0 collective-permute-start.3
  9.6 1.2 %shard_map.39 = (f32[256,256]{1,0:T(8,128)S(1)}, f32[256,256]{1,0:T(8,128)S(1)}) custom-call(s32[4,128]{1,0:T(4,128)S(1)} %collective-permute-done.1.refs_0_, s32[4,128]{1,0:T(4,128)S(1)} %shard_map.37.refs_0_.refs_1_, f32[256,256]{1,0:T(8,128)S(1)} %shard_map.38.refs_2_, bf16[4,2,128,128]{3,2,1,0:T(8,128)(2,1)S(1)} %copy-done, ...), custom_call_target="tpu_custom_call" | custom-call | flops 1610612736 | bytes 786432 | tf_op jit(solution)/shard_map/pallas_call | solution.py:140
  10.8 0.3 %collective-permute-done.3.refs_2_ = bf16[4,2,128,128]{3,2,1,0:T(8,128)(2,1)S(1)} collective-permute-done((bf16[4,2,128,128]{3,2,1,0:T(8,128)(2,1)S(1)}, bf16[4,2,128,128]{3,2,1,0:T(8,128)(2,1)S(1)}, u32[]{:S(2)}, u32[]{:S(2)}) %collective-permute-start.3) | collective-permute-done | bytes 262176 | tf_op jit(solution)/shard_map/ppermute | solution.py:166
  11.1 0.5 %shard_map.41 = (f32[64,256]{1,0:T(8,128)S(1)}, f32[64,256]{1,0:T(8,128)S(1)}, f32[64,256]{1,0:T(8,128)S(1)}, f32[64,256]{1,0:T(8,128)S(1)}) custom-call(s32[4,128]{1,0:T(4,128)S(1)} %collective-permute-done.1.refs_0_, f32[256,256]{1,0:T(8,128)S(1)} %get-tuple-element.28.refs_1_, bf16[4,2,128,128]{3,2,1,0:T(8,128)(2,1)S(1)} %collective-permute-done.3.refs_2_), custom_call_target="tpu_custom_call" | custom-call | flops 268435456 | bytes 262144 | tf_op jit(solution)/shard_map/pallas_call | solution.py:140
  11.6 2.7 %collective-permute-start.7 = (f32[64,256]{1,0:T(8,128)S(1)}, f32[64,256]{1,0:T(8,128)S(1)}, u32[]{:S(2)}, u32[]{:S(2)}) collective-permute-start(f32[64,256]{1,0:T(8,128)S(1)} %get-tuple-element.30), channel_id=1, source_target_pairs={{0,24},{4,12},{8,16},{12,4},{16,8},{20,28},{24,0},{28,20},{1,25},{... | collective-permute-start | bytes 196616 | tf_op jit(solution)/shard_map/ppermute | solution.py:185
  14.3 0.5 %collective-permute-start.8 = (f32[64,256]{1,0:T(8,128)S(1)}, f32[64,256]{1,0:T(8,128)S(1)}, u32[]{:S(2)}, u32[]{:S(2)}) collective-permute-start(f32[64,256]{1,0:T(8,128)S(1)} %get-tuple-element.31), channel_id=1, source_target_pairs={{0,16},{4,28},{8,24},{12,20},{16,0},{20,12},{24,8},{28,4},{1,17},{... | collective-permute-start | bytes 196616 | tf_op jit(solution)/shard_map/ppermute | solution.py:185
  14.8 0.4 %collective-permute-start.9 = (f32[64,256]{1,0:T(8,128)S(1)}, f32[64,256]{1,0:T(8,128)S(1)}, u32[]{:S(2)}, u32[]{:S(2)}) collective-permute-start(f32[64,256]{1,0:T(8,128)S(1)} %get-tuple-element.32), channel_id=1, source_target_pairs={{0,8},{4,20},{8,0},{12,28},{16,24},{20,4},{24,16},{28,12},{1,9},{5... | collective-permute-start | bytes 196616 | tf_op jit(solution)/shard_map/ppermute | solution.py:185
  15.2 0.5 %shard_map.40 = (f32[64,256]{1,0:T(8,128)S(1)}, f32[64,256]{1,0:T(8,128)S(1)}, f32[64,256]{1,0:T(8,128)S(1)}, f32[64,256]{1,0:T(8,128)S(1)}) custom-call(s32[4,128]{1,0:T(4,128)S(1)} %shard_map.37.refs_0_.refs_1_, f32[256,256]{1,0:T(8,128)S(1)} %get-tuple-element.23.refs_1_, bf16[4,2,128,128]{3,2,1,0:T(8,128)(2,1)S(1)} %collective-permute-done.3.refs_2_), custom_call_target="tpu_custom_call" | custom-call | flops 268435456 | bytes 262144 | tf_op jit(solution)/shard_map/pallas_call | solution.py:140
  15.7 2.7 %collective-permute-start.4 = (f32[64,256]{1,0:T(8,128)S(1)}, f32[64,256]{1,0:T(8,128)S(1)}, u32[]{:S(2)}, u32[]{:S(2)}) collective-permute-start(f32[64,256]{1,0:T(8,128)S(1)} %get-tuple-element.25), channel_id=1, source_target_pairs={{0,24},{4,12},{8,16},{12,4},{16,8},{20,28},{24,0},{28,20},{1,25},{... | collective-permute-start | bytes 196616 | tf_op jit(solution)/shard_map/ppermute | solution.py:185
  18.4 0.5 %collective-permute-start.5 = (f32[64,256]{1,0:T(8,128)S(1)}, f32[64,256]{1,0:T(8,128)S(1)}, u32[]{:S(2)}, u32[]{:S(2)}) collective-permute-start(f32[64,256]{1,0:T(8,128)S(1)} %get-tuple-element.26), channel_id=1, source_target_pairs={{0,16},{4,28},{8,24},{12,20},{16,0},{20,12},{24,8},{28,4},{1,17},{... | collective-permute-start | bytes 196616 | tf_op jit(solution)/shard_map/ppermute | solution.py:185
  18.9 0.0 collective-permute-done.7
  18.9 0.4 %collective-permute-start.6 = (f32[64,256]{1,0:T(8,128)S(1)}, f32[64,256]{1,0:T(8,128)S(1)}, u32[]{:S(2)}, u32[]{:S(2)}) collective-permute-start(f32[64,256]{1,0:T(8,128)S(1)} %get-tuple-element.27), channel_id=1, source_target_pairs={{0,8},{4,20},{8,0},{12,28},{16,24},{20,4},{24,16},{28,12},{1,9},{5... | collective-permute-start | bytes 196616 | tf_op jit(solution)/shard_map/ppermute | solution.py:185
  19.3 0.0 collective-permute-done.8
  19.3 0.0 collective-permute-done.9
  19.3 2.8 %collective-permute-start.10 = (f32[64,256]{1,0:T(8,128)S(1)}, f32[64,256]{1,0:T(8,128)S(1)}, u32[]{:S(2)}, u32[]{:S(2)}) collective-permute-start(f32[64,256]{1,0:T(8,128)S(1)} %add_add_fusion), channel_id=1, source_target_pairs={{0,2},{1,3},{2,0},{3,1},{4,6},{5,7},{6,4},{7,5},{8,10},{9,11},{10,... | collective-permute-start | bytes 196616 | tf_op jit(solution)/shard_map/ppermute | solution.py:166
  22.1 0.0 collective-permute-done.4
  22.1 0.8 %collective-permute-done.5 = f32[64,256]{1,0:T(8,128)S(1)} collective-permute-done((f32[64,256]{1,0:T(8,128)S(1)}, f32[64,256]{1,0:T(8,128)S(1)}, u32[]{:S(2)}, u32[]{:S(2)}) %collective-permute-start.5) | collective-permute-done | bytes 65568 | tf_op jit(solution)/shard_map/ppermute | solution.py:185
  22.9 0.2 collective-permute-done.6
  23.2 1.4 %collective-permute-done.10 = f32[64,256]{1,0:T(8,128)S(1)} collective-permute-done((f32[64,256]{1,0:T(8,128)S(1)}, f32[64,256]{1,0:T(8,128)S(1)}, u32[]{:S(2)}, u32[]{:S(2)}) %collective-permute-start.10) | collective-permute-done | bytes 65568 | tf_op jit(solution)/shard_map/ppermute | solution.py:166
  24.6 0.6 %copy.6 = f32[4,16,2,128]{3,1,0,2:T(8,128)} copy(f32[4,16,2,128]{3,2,1,0:T(2,128)S(1)} %reshape.3) | data formatting | bytes 131072 | tf_op jit(solution)/shard_map/reshape | solution.py:192
  (3 shorter events, 0.1 us)
Async XLA Ops:
  0.0 9.6 %collective-permute-start = (bf16[4,2,128,128]{3,2,1,0:T(8,128)(2,1)}, bf16[4,2,128,128]{3,2,1,0:T(8,128)(2,1)S(1)}, u32[]{:S(2)}, u32[]{:S(2)}) collective-permute-start(bf16[4,2,128,128]{3,2,1,0:T(8,128)(2,1)} %refs_3_.1), channel_id=1, source_target_pairs={{0,1},{1,0},{2,3},{3,2},{4,5},{5,4},{6,7},{7,6},{8,9},{9,8},{10,11... | collective-permute-start | bytes 786440 | tf_op jit(solution)/shard_map/ppermute | solution.py:166
  3.0 6.6 %collective-permute-start.2 = (bf16[4,2,128,128]{3,2,1,0:T(8,128)(2,1)}, bf16[4,2,128,128]{3,2,1,0:T(8,128)(2,1)S(1)}, u32[]{:S(2)}, u32[]{:S(2)}) collective-permute-start(bf16[4,2,128,128]{3,2,1,0:T(8,128)(2,1)} %refs_3_.1), channel_id=1, source_target_pairs={{0,4},{4,0},{8,12},{12,8},{16,20},{20,16},{24,28},{28,24},{1,5},{5... | collective-permute-start | bytes 786440 | tf_op jit(solution)/shard_map/ppermute | solution.py:166
  3.9 5.0 %collective-permute-start.1 = (s32[4,128]{1,0:T(4,128)S(1)}, s32[4,128]{1,0:T(4,128)S(1)}, u32[]{:S(2)}, u32[]{:S(2)}) collective-permute-start(s32[4,128]{1,0:T(4,128)S(1)} %shard_map.37.refs_0_.refs_1_), channel_id=1, source_target_pairs={{0,2},{1,3},{2,0},{3,1},{4,6},{5,7},{6,4},{7,5},{8,10},{9,11},{10,... | collective-permute-start | bytes 6152 | tf_op jit(solution)/shard_map/ppermute | solution.py:166
  6.5 0.9 %copy-start = (bf16[4,2,128,128]{3,2,1,0:T(8,128)(2,1)S(1)}, bf16[4,2,128,128]{3,2,1,0:T(8,128)(2,1)}, u32[]{:S(2)}) copy-start(bf16[4,2,128,128]{3,2,1,0:T(8,128)(2,1)} %refs_3_.1) | copy-start | bytes 786436
  9.6 1.5 %collective-permute-start.3 = (bf16[4,2,128,128]{3,2,1,0:T(8,128)(2,1)S(1)}, bf16[4,2,128,128]{3,2,1,0:T(8,128)(2,1)S(1)}, u32[]{:S(2)}, u32[]{:S(2)}) collective-permute-start(bf16[4,2,128,128]{3,2,1,0:T(8,128)(2,1)S(1)} %collective-permute-done.refs_5_), channel_id=1, source_target_pairs={{0,4},{4,0},{8,12},{12,8},{16,20},{20,16},{24,28},{28,24},{1,5},{5... | collective-permute-start | bytes 786440 | tf_op jit(solution)/shard_map/ppermute | solution.py:166
  11.6 7.3 %collective-permute-start.7 = (f32[64,256]{1,0:T(8,128)S(1)}, f32[64,256]{1,0:T(8,128)S(1)}, u32[]{:S(2)}, u32[]{:S(2)}) collective-permute-start(f32[64,256]{1,0:T(8,128)S(1)} %get-tuple-element.30), channel_id=1, source_target_pairs={{0,24},{4,12},{8,16},{12,4},{16,8},{20,28},{24,0},{28,20},{1,25},{... | collective-permute-start | bytes 196616 | tf_op jit(solution)/shard_map/ppermute | solution.py:185
  14.3 5.0 %collective-permute-start.8 = (f32[64,256]{1,0:T(8,128)S(1)}, f32[64,256]{1,0:T(8,128)S(1)}, u32[]{:S(2)}, u32[]{:S(2)}) collective-permute-start(f32[64,256]{1,0:T(8,128)S(1)} %get-tuple-element.31), channel_id=1, source_target_pairs={{0,16},{4,28},{8,24},{12,20},{16,0},{20,12},{24,8},{28,4},{1,17},{... | collective-permute-start | bytes 196616 | tf_op jit(solution)/shard_map/ppermute | solution.py:185
  14.8 4.5 %collective-permute-start.9 = (f32[64,256]{1,0:T(8,128)S(1)}, f32[64,256]{1,0:T(8,128)S(1)}, u32[]{:S(2)}, u32[]{:S(2)}) collective-permute-start(f32[64,256]{1,0:T(8,128)S(1)} %get-tuple-element.32), channel_id=1, source_target_pairs={{0,8},{4,20},{8,0},{12,28},{16,24},{20,4},{24,16},{28,12},{1,9},{5... | collective-permute-start | bytes 196616 | tf_op jit(solution)/shard_map/ppermute | solution.py:185
  15.7 6.4 %collective-permute-start.4 = (f32[64,256]{1,0:T(8,128)S(1)}, f32[64,256]{1,0:T(8,128)S(1)}, u32[]{:S(2)}, u32[]{:S(2)}) collective-permute-start(f32[64,256]{1,0:T(8,128)S(1)} %get-tuple-element.25), channel_id=1, source_target_pairs={{0,24},{4,12},{8,16},{12,4},{16,8},{20,28},{24,0},{28,20},{1,25},{... | collective-permute-start | bytes 196616 | tf_op jit(solution)/shard_map/ppermute | solution.py:185
  18.4 4.5 %collective-permute-start.5 = (f32[64,256]{1,0:T(8,128)S(1)}, f32[64,256]{1,0:T(8,128)S(1)}, u32[]{:S(2)}, u32[]{:S(2)}) collective-permute-start(f32[64,256]{1,0:T(8,128)S(1)} %get-tuple-element.26), channel_id=1, source_target_pairs={{0,16},{4,28},{8,24},{12,20},{16,0},{20,12},{24,8},{28,4},{1,17},{... | collective-permute-start | bytes 196616 | tf_op jit(solution)/shard_map/ppermute | solution.py:185
  18.9 4.3 %collective-permute-start.6 = (f32[64,256]{1,0:T(8,128)S(1)}, f32[64,256]{1,0:T(8,128)S(1)}, u32[]{:S(2)}, u32[]{:S(2)}) collective-permute-start(f32[64,256]{1,0:T(8,128)S(1)} %get-tuple-element.27), channel_id=1, source_target_pairs={{0,8},{4,20},{8,0},{12,28},{16,24},{20,4},{24,16},{28,12},{1,9},{5... | collective-permute-start | bytes 196616 | tf_op jit(solution)/shard_map/ppermute | solution.py:185
  19.3 5.2 %collective-permute-start.10 = (f32[64,256]{1,0:T(8,128)S(1)}, f32[64,256]{1,0:T(8,128)S(1)}, u32[]{:S(2)}, u32[]{:S(2)}) collective-permute-start(f32[64,256]{1,0:T(8,128)S(1)} %add_add_fusion), channel_id=1, source_target_pairs={{0,2},{1,3},{2,0},{3,1},{4,6},{5,7},{6,4},{7,5},{8,10},{9,11},{10,... | collective-permute-start | bytes 196616 | tf_op jit(solution)/shard_map/ppermute | solution.py:166

commit v7 on v6

--- a/solution.py
+++ b/solution.py
@@ -129,10 +129,12 @@
             for step in range(owners):
                 for tile in range(tiles):
                     at = tile * block + step * rows
-                    outs[group][step][tile * rows : (tile + 1) * rows, :] = sums[at : at + rows, :]
+                    for part in range(2):
+                        to = (part * tiles + tile) * rows
+                        outs[group][step][to : to + rows, :] = sums[at : at + rows, part * width : (part + 1) * width]
 
     if split:
-        out_shape = [jax.ShapeDtypeStruct((tiles * rows, 2 * width), jnp.float32)] * (len(groups) * owners)
+        out_shape = [jax.ShapeDtypeStruct((2 * tiles * rows, width), jnp.float32)] * (len(groups) * owners)
     else:
         out_shape = [jax.ShapeDtypeStruct((height, 2 * width), jnp.float32)] * len(groups)
     operands = [group[0] for group in groups] + [group[1] for group in groups if group[1] is not None] + sources
@@ -189,8 +191,7 @@
     done = collect(own_order, own)
     for other in others:
         done = done + other
-    done = done.reshape(tiles, rows, 2, width)
-    return jnp.transpose(done, (2, 0, 1, 3))
+    return done.reshape(2, tiles, rows, width)
 
 
 def solution(mesh):

time: 25.4 us -> 25.4 us (level)
  local copies, waits for them, and re-layouts: 1.62 us -> 0.95 us
  other arithmetic: 0.04 us -> 0.67 us
    reshape x2 -> x0, local copies, waits for them, and re-layouts: 0.67 us -> none  [body(): done = done.reshape(tiles, rows, 2, width)]
    add x1, other arithmetic: 0.02 us -> 0.65 us  [body(): done = done + other]
where the time goes in v7:
time: 25.4 us; the launch traced here: 25.2 us
  starting transfers between devices  15.5 us (61%)
  waiting for transfers between devices  4.41 us (17%)
  Pallas kernels  3.58 us (14%)
  local copies, waits for them, and re-layouts  0.95 us (4%)
  other arithmetic  0.67 us (3%)
    ppermute x5, starting transfers between devices, over(): return lax.ppermute(value, axis, [(i, i ^ flip) for i in range(size)])  8.42 us
    ppermute x6, starting transfers between devices, collect(): lax.ppermute(parts[step], 'rep', [(i, owner_of(rep, i, step)) for i in ra...  7.11 us
    ppermute x5, waiting for transfers between devices, over(): return lax.ppermute(value, axis, [(i, i ^ flip) for i in range(size)])  3.33 us
    pallas_call x4, Pallas kernels, partial_tiles(): pl.pallas_call(kernel, out_shape=out_shape, in_specs=[whole] * len(operan...  2.71 us
    ppermute x6, waiting for transfers between devices, collect(): lax.ppermute(parts[step], 'rep', [(i, owner_of(rep, i, step)) for i in ra...  1.08 us
    unnamed x2, local copies, waits for them, and re-layouts  0.95 us
    pallas_call x1, Pallas kernels, turned_order(): pl.pallas_call(kernel, out_shape=pltpu.VMEM(order.shape, order.dtype), in...  0.87 us
    add x1, other arithmetic, body(): done = done + other  0.65 us
  transfers between devices with their start and end apart: 11, of which 6 were waited for; matrix products, arithmetic and copies ran while one was open for 0% of the time, Pallas kernels for 12%

profile of v7, /device:TPU:0, one launch (start us, length us, event | category | flops | bytes accessed | tf_op | source)
XLA Modules:
  0.0 25.2 jit_solution(5619586390194657759)
XLA Ops:
  0.0 3.0 %collective-permute-start = (bf16[4,2,128,128]{3,2,1,0:T(8,128)(2,1)}, bf16[4,2,128,128]{3,2,1,0:T(8,128)(2,1)S(1)}, u32[]{:S(2)}, u32[]{:S(2)}) collective-permute-start(bf16[4,2,128,128]{3,2,1,0:T(8,128)(2,1)} %refs_3_.1), channel_id=1, source_target_pairs={{0,1},{1,0},{2,3},{3,2},{4,5},{5,4},{6,7},{7,6},{8,9},{9,8},{10,11... | collective-permute-start | bytes 786440 | tf_op jit(solution)/shard_map/ppermute | solution.py:168
  3.0 0.0 collective-permute-start.2
  3.0 0.9 %shard_map.37.refs_0_.refs_1_ = s32[4,128]{1,0:T(4,128)S(1)} custom-call(s32[4,128]{1,0:T(4,128)} %order_ref.1, s32[4]{0:T(128)} %offset_ref.1), custom_call_target="tpu_custom_call" | custom-call | tf_op jit(solution)/shard_map/pallas_call | solution.py:38
  3.9 2.6 %collective-permute-start.1 = (s32[4,128]{1,0:T(4,128)S(1)}, s32[4,128]{1,0:T(4,128)S(1)}, u32[]{:S(2)}, u32[]{:S(2)}) collective-permute-start(s32[4,128]{1,0:T(4,128)S(1)} %shard_map.37.refs_0_.refs_1_), channel_id=1, source_target_pairs={{0,2},{1,3},{2,0},{3,1},{4,6},{5,7},{6,4},{7,5},{8,10},{9,11},{10,... | collective-permute-start | bytes 6152 | tf_op jit(solution)/shard_map/ppermute | solution.py:168
  6.5 0.0 copy-start
  6.5 0.9 %copy-done = bf16[4,2,128,128]{3,2,1,0:T(8,128)(2,1)S(1)} copy-done((bf16[4,2,128,128]{3,2,1,0:T(8,128)(2,1)S(1)}, bf16[4,2,128,128]{3,2,1,0:T(8,128)(2,1)}, u32[]{:S(2)}) %copy-start) | copy-done | bytes 262168
  7.4 0.5 %shard_map.38.refs_2_ = f32[256,256]{1,0:T(8,128)S(1)} custom-call(s32[4,128]{1,0:T(4,128)S(1)} %shard_map.37.refs_0_.refs_1_, bf16[4,2,128,128]{3,2,1,0:T(8,128)(2,1)S(1)} %copy-done), custom_call_target="tpu_custom_call" | custom-call | flops 268435456 | bytes 262144 | tf_op jit(solution)/shard_map/pallas_call | solution.py:142
  8.0 1.0 %collective-permute-done.1.refs_0_ = s32[4,128]{1,0:T(4,128)S(1)} collective-permute-done((s32[4,128]{1,0:T(4,128)S(1)}, s32[4,128]{1,0:T(4,128)S(1)}, u32[]{:S(2)}, u32[]{:S(2)}) %collective-permute-start.1) | collective-permute-done | bytes 2080 | tf_op jit(solution)/shard_map/ppermute | solution.py:168
  8.9 0.7 %collective-permute-done.refs_5_ = bf16[4,2,128,128]{3,2,1,0:T(8,128)(2,1)S(1)} collective-permute-done((bf16[4,2,128,128]{3,2,1,0:T(8,128)(2,1)}, bf16[4,2,128,128]{3,2,1,0:T(8,128)(2,1)S(1)}, u32[]{:S(2)}, u32[]{:S(2)}) %collective-permute-start) | collective-permute-done | bytes 262176 | tf_op jit(solution)/shard_map/ppermute | solution.py:168
  9.6 0.0 collective-permute-done.2.refs_4_
  9.6 0.0 collective-permute-start.3
  9.6 1.2 %shard_map.39 = (f32[256,256]{1,0:T(8,128)S(1)}, f32[256,256]{1,0:T(8,128)S(1)}) custom-call(s32[4,128]{1,0:T(4,128)S(1)} %collective-permute-done.1.refs_0_, s32[4,128]{1,0:T(4,128)S(1)} %shard_map.37.refs_0_.refs_1_, f32[256,256]{1,0:T(8,128)S(1)} %shard_map.38.refs_2_, bf16[4,2,128,128]{3,2,1,0:T(8,128)(2,1)S(1)} %copy-done, ...), custom_call_target="tpu_custom_call" | custom-call | flops 1610612736 | bytes 786432 | tf_op jit(solution)/shard_map/pallas_call | solution.py:142
  10.8 0.3 %collective-permute-done.3.refs_2_ = bf16[4,2,128,128]{3,2,1,0:T(8,128)(2,1)S(1)} collective-permute-done((bf16[4,2,128,128]{3,2,1,0:T(8,128)(2,1)S(1)}, bf16[4,2,128,128]{3,2,1,0:T(8,128)(2,1)S(1)}, u32[]{:S(2)}, u32[]{:S(2)}) %collective-permute-start.3) | collective-permute-done | bytes 262176 | tf_op jit(solution)/shard_map/ppermute | solution.py:168
  11.1 0.5 %shard_map.41 = (f32[128,128]{1,0:T(8,128)S(1)}, f32[128,128]{1,0:T(8,128)S(1)}, f32[128,128]{1,0:T(8,128)S(1)}, f32[128,128]{1,0:T(8,128)S(1)}) custom-call(s32[4,128]{1,0:T(4,128)S(1)} %collective-permute-done.1.refs_0_, f32[256,256]{1,0:T(8,128)S(1)} %get-tuple-element.28.refs_1_, bf16[4,2,128,128]{3,2,1,0:T(8,128)(2,1)S(1)} %collective-permute-done.3.refs_2_), custom_call_target="tpu_custom_call" | custom-call | flops 268435456 | bytes 262144 | tf_op jit(solution)/shard_map/pallas_call | solution.py:142
  11.6 2.7 %collective-permute-start.7 = (f32[128,128]{1,0:T(8,128)S(1)}, f32[128,128]{1,0:T(8,128)S(1)}, u32[]{:S(2)}, u32[]{:S(2)}) collective-permute-start(f32[128,128]{1,0:T(8,128)S(1)} %get-tuple-element.30), channel_id=1, source_target_pairs={{0,24},{4,12},{8,16},{12,4},{16,8},{20,28},{24,0},{28,20},{1,25},{... | collective-permute-start | bytes 196616 | tf_op jit(solution)/shard_map/ppermute | solution.py:187
  14.3 0.5 %collective-permute-start.8 = (f32[128,128]{1,0:T(8,128)S(1)}, f32[128,128]{1,0:T(8,128)S(1)}, u32[]{:S(2)}, u32[]{:S(2)}) collective-permute-start(f32[128,128]{1,0:T(8,128)S(1)} %get-tuple-element.31), channel_id=1, source_target_pairs={{0,16},{4,28},{8,24},{12,20},{16,0},{20,12},{24,8},{28,4},{1,17},{... | collective-permute-start | bytes 196616 | tf_op jit(solution)/shard_map/ppermute | solution.py:187
  14.8 0.4 %collective-permute-start.9 = (f32[128,128]{1,0:T(8,128)S(1)}, f32[128,128]{1,0:T(8,128)S(1)}, u32[]{:S(2)}, u32[]{:S(2)}) collective-permute-start(f32[128,128]{1,0:T(8,128)S(1)} %get-tuple-element.32), channel_id=1, source_target_pairs={{0,8},{4,20},{8,0},{12,28},{16,24},{20,4},{24,16},{28,12},{1,9},{5... | collective-permute-start | bytes 196616 | tf_op jit(solution)/shard_map/ppermute | solution.py:187
  15.2 0.5 %shard_map.40 = (f32[128,128]{1,0:T(8,128)S(1)}, f32[128,128]{1,0:T(8,128)S(1)}, f32[128,128]{1,0:T(8,128)S(1)}, f32[128,128]{1,0:T(8,128)S(1)}) custom-call(s32[4,128]{1,0:T(4,128)S(1)} %shard_map.37.refs_0_.refs_1_, f32[256,256]{1,0:T(8,128)S(1)} %get-tuple-element.23.refs_1_, bf16[4,2,128,128]{3,2,1,0:T(8,128)(2,1)S(1)} %collective-permute-done.3.refs_2_), custom_call_target="tpu_custom_call" | custom-call | flops 268435456 | bytes 262144 | tf_op jit(solution)/shard_map/pallas_call | solution.py:142
  15.7 2.7 %collective-permute-start.4 = (f32[128,128]{1,0:T(8,128)S(1)}, f32[128,128]{1,0:T(8,128)S(1)}, u32[]{:S(2)}, u32[]{:S(2)}) collective-permute-start(f32[128,128]{1,0:T(8,128)S(1)} %get-tuple-element.25), channel_id=1, source_target_pairs={{0,24},{4,12},{8,16},{12,4},{16,8},{20,28},{24,0},{28,20},{1,25},{... | collective-permute-start | bytes 196616 | tf_op jit(solution)/shard_map/ppermute | solution.py:187
  18.4 0.5 %collective-permute-start.5 = (f32[128,128]{1,0:T(8,128)S(1)}, f32[128,128]{1,0:T(8,128)S(1)}, u32[]{:S(2)}, u32[]{:S(2)}) collective-permute-start(f32[128,128]{1,0:T(8,128)S(1)} %get-tuple-element.26), channel_id=1, source_target_pairs={{0,16},{4,28},{8,24},{12,20},{16,0},{20,12},{24,8},{28,4},{1,17},{... | collective-permute-start | bytes 196616 | tf_op jit(solution)/shard_map/ppermute | solution.py:187
  18.9 0.0 collective-permute-done.7
  18.9 0.4 %collective-permute-start.6 = (f32[128,128]{1,0:T(8,128)S(1)}, f32[128,128]{1,0:T(8,128)S(1)}, u32[]{:S(2)}, u32[]{:S(2)}) collective-permute-start(f32[128,128]{1,0:T(8,128)S(1)} %get-tuple-element.27), channel_id=1, source_target_pairs={{0,8},{4,20},{8,0},{12,28},{16,24},{20,4},{24,16},{28,12},{1,9},{5... | collective-permute-start | bytes 196616 | tf_op jit(solution)/shard_map/ppermute | solution.py:187
  19.3 0.0 collective-permute-done.8
  19.3 0.0 collective-permute-done.9
  19.3 2.8 %collective-permute-start.10 = (f32[128,128]{1,0:T(8,128)S(1)}, f32[128,128]{1,0:T(8,128)S(1)}, u32[]{:S(2)}, u32[]{:S(2)}) collective-permute-start(f32[128,128]{1,0:T(8,128)S(1)} %add_add_fusion), channel_id=1, source_target_pairs={{0,2},{1,3},{2,0},{3,1},{4,6},{5,7},{6,4},{7,5},{8,10},{9,11},{10,... | collective-permute-start | bytes 196616 | tf_op jit(solution)/shard_map/ppermute | solution.py:168
  22.1 0.0 collective-permute-done.4
  22.1 0.8 %collective-permute-done.5 = f32[128,128]{1,0:T(8,128)S(1)} collective-permute-done((f32[128,128]{1,0:T(8,128)S(1)}, f32[128,128]{1,0:T(8,128)S(1)}, u32[]{:S(2)}, u32[]{:S(2)}) %collective-permute-start.5) | collective-permute-done | bytes 65568 | tf_op jit(solution)/shard_map/ppermute | solution.py:187
  22.9 0.2 collective-permute-done.6
  23.2 1.4 %collective-permute-done.10 = f32[128,128]{1,0:T(8,128)S(1)} collective-permute-done((f32[128,128]{1,0:T(8,128)S(1)}, f32[128,128]{1,0:T(8,128)S(1)}, u32[]{:S(2)}, u32[]{:S(2)}) %collective-permute-start.10) | collective-permute-done | bytes 65568 | tf_op jit(solution)/shard_map/ppermute | solution.py:168
  24.5 0.7 %add_add_fusion.1 = f32[128,128]{1,0:T(8,128)} fusion(f32[128,128]{1,0:T(8,128)S(1)} %collective-permute-done.10, f32[128,128]{1,0:T(8,128)S(1)} %collective-permute-done.6, f32[128,128]{1,0:T(8,128)S(1)} %collective-permute-done.5, f32[128,128]{1,0:T(8,128)S(1)} %get-tuple-element.24, f32[128,128]{1,0:T(8,128)S(1)} %collective-permute-done.4), kind=kLoop, calls=%fused_computation.1 | loop fusion | flops 65536 | bytes 393216 | tf_op jit(solution)/shard_map/add | solution.py:193
  (1 shorter events, 0.0 us)
Async XLA Ops:
  0.0 9.6 %collective-permute-start = (bf16[4,2,128,128]{3,2,1,0:T(8,128)(2,1)}, bf16[4,2,128,128]{3,2,1,0:T(8,128)(2,1)S(1)}, u32[]{:S(2)}, u32[]{:S(2)}) collective-permute-start(bf16[4,2,128,128]{3,2,1,0:T(8,128)(2,1)} %refs_3_.1), channel_id=1, source_target_pairs={{0,1},{1,0},{2,3},{3,2},{4,5},{5,4},{6,7},{7,6},{8,9},{9,8},{10,11... | collective-permute-start | bytes 786440 | tf_op jit(solution)/shard_map/ppermute | solution.py:168
  3.0 6.6 %collective-permute-start.2 = (bf16[4,2,128,128]{3,2,1,0:T(8,128)(2,1)}, bf16[4,2,128,128]{3,2,1,0:T(8,128)(2,1)S(1)}, u32[]{:S(2)}, u32[]{:S(2)}) collective-permute-start(bf16[4,2,128,128]{3,2,1,0:T(8,128)(2,1)} %refs_3_.1), channel_id=1, source_target_pairs={{0,4},{4,0},{8,12},{12,8},{16,20},{20,16},{24,28},{28,24},{1,5},{5... | collective-permute-start | bytes 786440 | tf_op jit(solution)/shard_map/ppermute | solution.py:168
  3.9 5.0 %collective-permute-start.1 = (s32[4,128]{1,0:T(4,128)S(1)}, s32[4,128]{1,0:T(4,128)S(1)}, u32[]{:S(2)}, u32[]{:S(2)}) collective-permute-start(s32[4,128]{1,0:T(4,128)S(1)} %shard_map.37.refs_0_.refs_1_), channel_id=1, source_target_pairs={{0,2},{1,3},{2,0},{3,1},{4,6},{5,7},{6,4},{7,5},{8,10},{9,11},{10,... | collective-permute-start | bytes 6152 | tf_op jit(solution)/shard_map/ppermute | solution.py:168
  6.5 0.9 %copy-start = (bf16[4,2,128,128]{3,2,1,0:T(8,128)(2,1)S(1)}, bf16[4,2,128,128]{3,2,1,0:T(8,128)(2,1)}, u32[]{:S(2)}) copy-start(bf16[4,2,128,128]{3,2,1,0:T(8,128)(2,1)} %refs_3_.1) | copy-start | bytes 786436
  9.6 1.5 %collective-permute-start.3 = (bf16[4,2,128,128]{3,2,1,0:T(8,128)(2,1)S(1)}, bf16[4,2,128,128]{3,2,1,0:T(8,128)(2,1)S(1)}, u32[]{:S(2)}, u32[]{:S(2)}) collective-permute-start(bf16[4,2,128,128]{3,2,1,0:T(8,128)(2,1)S(1)} %collective-permute-done.refs_5_), channel_id=1, source_target_pairs={{0,4},{4,0},{8,12},{12,8},{16,20},{20,16},{24,28},{28,24},{1,5},{5... | collective-permute-start | bytes 786440 | tf_op jit(solution)/shard_map/ppermute | solution.py:168
  11.6 7.3 %collective-permute-start.7 = (f32[128,128]{1,0:T(8,128)S(1)}, f32[128,128]{1,0:T(8,128)S(1)}, u32[]{:S(2)}, u32[]{:S(2)}) collective-permute-start(f32[128,128]{1,0:T(8,128)S(1)} %get-tuple-element.30), channel_id=1, source_target_pairs={{0,24},{4,12},{8,16},{12,4},{16,8},{20,28},{24,0},{28,20},{1,25},{... | collective-permute-start | bytes 196616 | tf_op jit(solution)/shard_map/ppermute | solution.py:187
  14.3 5.0 %collective-permute-start.8 = (f32[128,128]{1,0:T(8,128)S(1)}, f32[128,128]{1,0:T(8,128)S(1)}, u32[]{:S(2)}, u32[]{:S(2)}) collective-permute-start(f32[128,128]{1,0:T(8,128)S(1)} %get-tuple-element.31), channel_id=1, source_target_pairs={{0,16},{4,28},{8,24},{12,20},{16,0},{20,12},{24,8},{28,4},{1,17},{... | collective-permute-start | bytes 196616 | tf_op jit(solution)/shard_map/ppermute | solution.py:187
  14.8 4.5 %collective-permute-start.9 = (f32[128,128]{1,0:T(8,128)S(1)}, f32[128,128]{1,0:T(8,128)S(1)}, u32[]{:S(2)}, u32[]{:S(2)}) collective-permute-start(f32[128,128]{1,0:T(8,128)S(1)} %get-tuple-element.32), channel_id=1, source_target_pairs={{0,8},{4,20},{8,0},{12,28},{16,24},{20,4},{24,16},{28,12},{1,9},{5... | collective-permute-start | bytes 196616 | tf_op jit(solution)/shard_map/ppermute | solution.py:187
  15.7 6.4 %collective-permute-start.4 = (f32[128,128]{1,0:T(8,128)S(1)}, f32[128,128]{1,0:T(8,128)S(1)}, u32[]{:S(2)}, u32[]{:S(2)}) collective-permute-start(f32[128,128]{1,0:T(8,128)S(1)} %get-tuple-element.25), channel_id=1, source_target_pairs={{0,24},{4,12},{8,16},{12,4},{16,8},{20,28},{24,0},{28,20},{1,25},{... | collective-permute-start | bytes 196616 | tf_op jit(solution)/shard_map/ppermute | solution.py:187
  18.4 4.5 %collective-permute-start.5 = (f32[128,128]{1,0:T(8,128)S(1)}, f32[128,128]{1,0:T(8,128)S(1)}, u32[]{:S(2)}, u32[]{:S(2)}) collective-permute-start(f32[128,128]{1,0:T(8,128)S(1)} %get-tuple-element.26), channel_id=1, source_target_pairs={{0,16},{4,28},{8,24},{12,20},{16,0},{20,12},{24,8},{28,4},{1,17},{... | collective-permute-start | bytes 196616 | tf_op jit(solution)/shard_map/ppermute | solution.py:187
  18.9 4.3 %collective-permute-start.6 = (f32[128,128]{1,0:T(8,128)S(1)}, f32[128,128]{1,0:T(8,128)S(1)}, u32[]{:S(2)}, u32[]{:S(2)}) collective-permute-start(f32[128,128]{1,0:T(8,128)S(1)} %get-tuple-element.27), channel_id=1, source_target_pairs={{0,8},{4,20},{8,0},{12,28},{16,24},{20,4},{24,16},{28,12},{1,9},{5... | collective-permute-start | bytes 196616 | tf_op jit(solution)/shard_map/ppermute | solution.py:187
  19.3 5.2 %collective-permute-start.10 = (f32[128,128]{1,0:T(8,128)S(1)}, f32[128,128]{1,0:T(8,128)S(1)}, u32[]{:S(2)}, u32[]{:S(2)}) collective-permute-start(f32[128,128]{1,0:T(8,128)S(1)} %add_add_fusion), channel_id=1, source_target_pairs={{0,2},{1,3},{2,0},{3,1},{4,6},{5,7},{6,4},{7,5},{8,10},{9,11},{10,... | collective-permute-start | bytes 196616 | tf_op jit(solution)/shard_map/ppermute | solution.py:168
